TPU v7x, 128 devices: a whole 4x4x4 slice. The times are simulated.
128 devices in a mesh: section: 4 (over x), dp: 32 (over z, y, core).
Axes of the slice: x: 4, y: 4, z: 4, core: 2. Of those that a mesh axis runs over, the one named last changes fastest.
Arguments:
- tokens: bfloat16 [2, 4096, 5120], P(None, 'dp'), may hold values from -26 to 26
- cotangent: bfloat16 [2, 4096, 5120], P(None, 'dp'), may hold values from -0.59765625 to 0.59765625
- norm_gain: float32 [4, 5120], P('section'), may hold values from 0.25 to 1.75
- value_weight: bfloat16 [4, 5120, 512], P('section'), may hold values from -2 to 2
- out_weight: bfloat16 [4, 512, 5120], P('section'), may hold values from -2 to 2
- adapter_down: bfloat16 [4, 128, 5120, 64], P('section', None, 'dp'), may hold values from -0.078125 to 0.078125
- adapter_up: bfloat16 [4, 128, 512, 64], P('section', None, 'dp'), may hold values from -0.75 to 0.75
- criterion: int32 [2, 32], replicated, may hold values from 0 to 127
- slot_of: int32 [128], replicated, may hold values from 0 to 127, each once
Outputs:
- grad_down: float32 [4, 128, 5120, 64], P('section', None, 'dp')
- grad_up: float32 [4, 128, 512, 64], P('section', None, 'dp')
Inputs may be any that keep to these rules, and one draw needn't show every extreme that they name: Each block's criterion id; some criteria are far more common than others, and one criterion may serve many blocks. `slot_of`: each of 0 to 127 once.
All inputs are finite; a program needn't handle non-finite values.
Results may differ from a plain program's by a relative error of at most 0.015.
Values may be sent and summed in bfloat16 or wider, within the bound.
A program may use at most 192 MiB of HBM per device.

v0:
```python
import jax
import jax.numpy as jnp
from jax import lax
from jax.sharding import PartitionSpec as P

epsilon = 1e-06


def passed_along(value, axis, steps):
    count = lax.axis_size(axis)
    first, last = (max(0, -steps), min(count, count - steps))
    return lax.ppermute(value, axis, [(source, source + steps) for source in range(first, last)])


def normalize(hidden, gains):
    widened = hidden.astype(jnp.float32)
    inverse = lax.rsqrt(jnp.mean(widened * widened, axis=-1, keepdims=True) + epsilon)
    return ((widened * inverse * gains).astype(jnp.bfloat16), inverse)


def forward_section(hidden, gains, w_value, w_out, down_panel, up_panel):
    normed, inverse = normalize(hidden, gains)
    blocks = down_panel.shape[0]
    grouped = normed.reshape(blocks, -1, normed.shape[-1])
    low_rank = jnp.einsum(
        "btd,bdr->btr", grouped, down_panel, preferred_element_type=jnp.float32
    ).astype(jnp.bfloat16)
    lifted = jnp.einsum("btr,bkr->btk", low_rank, up_panel, preferred_element_type=jnp.float32)
    lifted = lifted.reshape(hidden.shape[0], -1)
    values = (jnp.dot(normed, w_value, preferred_element_type=jnp.float32) + lifted).astype(
        jnp.bfloat16
    )
    mixed = hidden.astype(jnp.float32) + jnp.dot(values, w_out, preferred_element_type=jnp.float32)
    return mixed.astype(jnp.bfloat16)


def backward_section(hidden, gradient, gains, w_value, w_out, down_panel, up_panel):
    normed, inverse = normalize(hidden, gains)
    blocks = down_panel.shape[0]
    grouped = normed.reshape(blocks, -1, normed.shape[-1])
    low_rank = jnp.einsum(
        "btd,bdr->btr", grouped, down_panel, preferred_element_type=jnp.float32
    ).astype(jnp.bfloat16)
    grad_value = jnp.einsum(
        "td,kd->tk", gradient, w_out, preferred_element_type=jnp.float32
    ).astype(jnp.bfloat16)
    grad_groups = grad_value.reshape(blocks, -1, grad_value.shape[-1])
    grad_low = jnp.einsum(
        "btk,bkr->btr", grad_groups, up_panel, preferred_element_type=jnp.float32
    ).astype(jnp.bfloat16)
    pulled = jnp.einsum("btr,bdr->btd", grad_low, down_panel, preferred_element_type=jnp.float32)
    pulled = pulled.reshape(hidden.shape[0], -1)
    grad_norm = (
        jnp.einsum("tk,dk->td", grad_value, w_value, preferred_element_type=jnp.float32) + pulled
    )
    scaled = grad_norm * gains
    widened = hidden.astype(jnp.float32)
    moment = jnp.mean(scaled * widened, axis=-1, keepdims=True)
    grad_hidden = (
        gradient.astype(jnp.float32)
        + inverse * scaled
        - widened * inverse * inverse * inverse * moment
    )
    return (grad_hidden.astype(jnp.bfloat16), grouped, low_rank, grad_groups, grad_low)


def pick_step(store, position):
    return lax.dynamic_index_in_dim(store, position, 0, keepdims=False)


def put_step(store, item, position, live_step):
    return jnp.where(live_step, lax.dynamic_update_index_in_dim(store, item, position, 0), store)


def on_device(
    tokens,
    cotangent,
    norm_gain,
    value_weight,
    out_weight,
    adapter_down,
    adapter_up,
    criterion,
    slot_of,
):
    sections = lax.axis_size("section")
    data_count = lax.axis_size("dp")
    section_index = lax.axis_index("section")
    micro_count = tokens.shape[0]
    row_count = tokens.shape[1]
    model_width = tokens.shape[2]
    per_device = criterion.shape[1] // data_count
    gains = norm_gain[0]
    w_value = value_weight[0]
    w_out = out_weight[0]
    down_table = adapter_down[0]
    up_table = adapter_up[0]
    table_size = down_table.shape[0]
    rank_width = down_table.shape[2]
    value_width = up_table.shape[1] * data_count
    slots = slot_of[criterion]
    down_store = jnp.zeros((micro_count, per_device, model_width, rank_width), jnp.bfloat16)
    up_store = jnp.zeros((micro_count, per_device, value_width, rank_width), jnp.bfloat16)
    hidden_store = jnp.zeros((micro_count, row_count, model_width), jnp.bfloat16)
    carried = jnp.zeros((row_count, model_width), jnp.bfloat16)
    steps_total = micro_count + sections - 1
    for tick_index in range(steps_total):
        micro_index = tick_index - section_index
        live_step = (micro_index >= 0) & (micro_index < micro_count)
        safe_index = jnp.clip(micro_index, 0, micro_count - 1)
        picked = pick_step(slots, safe_index)
        down_panel, up_panel = (
            lax.all_to_all(down_table[picked], "dp", split_axis=0, concat_axis=1, tiled=True),
            lax.all_to_all(up_table[picked], "dp", split_axis=0, concat_axis=1, tiled=True),
        )
        down_store = put_step(down_store, down_panel, safe_index, live_step)
        up_store = put_step(up_store, up_panel, safe_index, live_step)
        first_input = pick_step(tokens, safe_index)
        hidden = jnp.where(section_index == 0, first_input, carried)
        hidden_store = put_step(hidden_store, hidden, safe_index, live_step)
        result = forward_section(hidden, gains, w_value, w_out, down_panel, up_panel)
        if tick_index < steps_total - 1:
            carried = passed_along(result, "section", 1)
    grad_down = jnp.zeros(down_table.shape, jnp.float32)
    grad_up = jnp.zeros(up_table.shape, jnp.float32)
    table_rows = jnp.arange(table_size, dtype=jnp.int32)
    carried = jnp.zeros((row_count, model_width), jnp.bfloat16)
    for tick_index in range(steps_total):
        micro_index = tick_index - (sections - 1 - section_index)
        live_step = (micro_index >= 0) & (micro_index < micro_count)
        safe_index = jnp.clip(micro_index, 0, micro_count - 1)
        hidden = pick_step(hidden_store, safe_index)
        down_panel = pick_step(down_store, safe_index)
        up_panel = pick_step(up_store, safe_index)
        last_input = pick_step(cotangent, safe_index)
        gradient = jnp.where(section_index == sections - 1, last_input, carried)
        grad_hidden, grouped, low_rank, grad_groups, grad_low = backward_section(
            hidden, gradient, gains, w_value, w_out, down_panel, up_panel
        )
        if tick_index < steps_total - 1:
            carried = passed_along(grad_hidden, "section", -1)
        slice_norm, slice_grad = (
            lax.all_to_all(grouped, "dp", split_axis=2, concat_axis=0, tiled=True),
            lax.all_to_all(grad_groups, "dp", split_axis=2, concat_axis=0, tiled=True),
        )
        every_low, every_grad = (
            lax.all_gather(low_rank, "dp", axis=0, tiled=True),
            lax.all_gather(grad_low, "dp", axis=0, tiled=True),
        )
        owner_down = jnp.einsum(
            "btd,btr->bdr", slice_norm, every_grad, preferred_element_type=jnp.float32
        )
        owner_up = jnp.einsum(
            "btk,btr->bkr", slice_grad, every_low, preferred_element_type=jnp.float32
        )
        picked = pick_step(slots, safe_index)
        selector = jnp.where(
            live_step, (table_rows[:, None] == picked[None, :]).astype(jnp.float32), 0.0
        )
        block_total = picked.shape[0]
        grad_down = grad_down + jnp.dot(
            selector, owner_down.reshape(block_total, -1), precision=lax.Precision.HIGHEST
        ).reshape(grad_down.shape)
        grad_up = grad_up + jnp.dot(
            selector, owner_up.reshape(block_total, -1), precision=lax.Precision.HIGHEST
        ).reshape(grad_up.shape)
    return (grad_down[None], grad_up[None])


def solution(mesh):
    return jax.shard_map(
        on_device,
        mesh=mesh,
        in_specs=(
            P(None, "dp", None),
            P(None, "dp", None),
            P("section", None),
            P("section", None, None),
            P("section", None, None),
            P("section", None, "dp", None),
            P("section", None, "dp", None),
            P(),
            P(),
        ),
        out_specs=(P("section", None, "dp", None), P("section", None, "dp", None)),
        check_vma=False,
    )
```

profile of v0, /device:TPU:1, one launch (start us, length us, event | category | flops | bytes accessed | tf_op | source)
XLA Modules:
  0.0 1181.9 jit_solution(15930769130801176882)
XLA Ops:
  5.2 9.6 all-to-all-start.1
  117.8 16.2 %all-to-all-done = bf16[32,160,64]{1,2,0:T(8,128)(2,1)} async-done(((bf16[32,160,64]{1,2,0:T(8,128)(2,1)}), bf16[32,160,64]{1,2,0:T(8,128)(2,1)}, u32[]{:S(2)}, u32[]{:S(2)}) %all-to-all-start) | async-done | bytes 655392 | tf_op jit(solution)/shard_map/all_to_all | solution.py:113
  180.9 8.2 all-to-all-start.11
  215.4 8.7 all-to-all-start.6
  274.6 19.2 %collective-permute-done.2 = bf16[128,5120]{1,0:T(8,128)(2,1)} collective-permute-done((bf16[128,5120]{1,0:T(8,128)(2,1)}, bf16[128,5120]{1,0:T(8,128)(2,1)}, u32[]{:S(2)}, u32[]{:S(2)}) %collective-permute-start.2) | collective-permute-done | bytes 1310752 | tf_op jit(solution)/shard_map/ppermute | solution.py:12
  313.2 24.8 %collective-permute-done.3 = bf16[128,5120]{1,0:T(8,128)(2,1)S(1)} collective-permute-done((bf16[128,5120]{1,0:T(8,128)(2,1)}, bf16[128,5120]{1,0:T(8,128)(2,1)S(1)}, u32[]{:S(2)}, u32[]{:S(2)}) %collective-permute-start.3) | collective-permute-done | bytes 1310752 | tf_op jit(solution)/shard_map/ppermute | solution.py:12
  345.5 29.4 %collective-permute-done.4 = bf16[128,5120]{1,0:T(8,128)(2,1)S(1)} collective-permute-done((bf16[128,5120]{1,0:T(8,128)(2,1)S(1)}, bf16[128,5120]{1,0:T(8,128)(2,1)S(1)}, u32[]{:S(2)}, u32[]{:S(2)}) %collective-permute-start.4) | collective-permute-done | bytes 1310752 | tf_op jit(solution)/shard_map/ppermute | solution.py:12
  383.3 28.0 %collective-permute-done.5 = bf16[128,5120]{1,0:T(8,128)(2,1)S(1)} collective-permute-done((bf16[128,5120]{1,0:T(8,128)(2,1)S(1)}, bf16[128,5120]{1,0:T(8,128)(2,1)S(1)}, u32[]{:S(2)}, u32[]{:S(2)}) %collective-permute-start.5) | collective-permute-done | bytes 1310752 | tf_op jit(solution)/shard_map/ppermute | solution.py:12
  425.2 9.9 all-to-all-start.15
  435.7 27.8 %all-gather = bf16[4096,64]{0,1:T(8,128)(2,1)} all-gather(bf16[128,64]{0,1:T(8,128)(2,1)S(1)} %copy-done.44), channel_id=2, replica_groups=mesh['section'=4,'dp'=32] {'dp'}, dimensions={0}, use_global_device_ids=true | all-gather | bytes 540672 | tf_op jit(solution)/shard_map/all_gather | solution.py:148
  473.3 27.7 %all-gather.1 = bf16[4096,64]{0,1:T(8,128)(2,1)} all-gather(bf16[128,64]{0,1:T(8,128)(2,1)S(1)} %convolution_convert_fusion.3), channel_id=3, replica_groups=mesh['section'=4,'dp'=32] {'dp'}, dimensions={0}, use_global_device_ids=true | all-gather | bytes 540672 | tf_op jit(solution)/shard_map/all_gather | solution.py:148
  509.2 25.3 %all-gather.2 = bf16[4096,64]{0,1:T(8,128)(2,1)S(1)} all-gather(bf16[128,64]{0,1:T(8,128)(2,1)S(1)} %convolution_convert_fusion.2), channel_id=4, replica_groups=mesh['section'=4,'dp'=32] {'dp'}, dimensions={0}, use_global_device_ids=true | all-gather | bytes 540672 | tf_op jit(solution)/shard_map/all_gather | solution.py:148
  566.6 29.9 %reduce.1 = bf16[5120,128]{1,0:T(8,128)(2,1)} reduce(bf16[5120,1,128]{2,1,0:T(2,128)(2,1)} %bitcast.623, bf16[]{:T(256)} %broadcast.422), dimensions={1}, to_apply=%bitcast.503.reduce_sub_computation | reduce | bytes 2621442
  620.4 29.0 %reduce.2 = bf16[5120,128]{1,0:T(8,128)(2,1)S(1)} reduce(bf16[5120,1,128]{2,1,0:T(2,128)(2,1)} %bitcast.624, bf16[]{:T(256)} %broadcast.422), dimensions={1}, to_apply=%bitcast.505.reduce_sub_computation | reduce | bytes 2621442
  654.6 29.9 %reduce.4 = bf16[5120,128]{1,0:T(8,128)(2,1)} reduce(bf16[5120,1,128]{2,1,0:T(2,128)(2,1)} %bitcast.625, bf16[]{:T(256)} %broadcast.422), dimensions={1}, to_apply=%bitcast.509.reduce_sub_computation | reduce | bytes 2621442
  696.0 37.9 %all-gather.3 = bf16[4096,64]{0,1:T(8,128)(2,1)} all-gather(bf16[128,64]{0,1:T(8,128)(2,1)S(1)} %convolution_convert_fusion.1), channel_id=5, replica_groups=mesh['section'=4,'dp'=32] {'dp'}, dimensions={0}, use_global_device_ids=true | all-gather | bytes 540672 | tf_op jit(solution)/shard_map/all_gather | solution.py:148
  735.6 26.5 %all-gather.8 = bf16[4096,64]{0,1:T(8,128)(2,1)} all-gather(bf16[128,64]{0,1:T(8,128)(2,1)S(1)} %fusion.166), channel_id=10, replica_groups=mesh['section'=4,'dp'=32] {'dp'}, dimensions={0}, use_global_device_ids=true | all-gather | bytes 540672 | tf_op jit(solution)/shard_map/all_gather | solution.py:147
  773.0 37.9 %all-gather.7 = bf16[4096,64]{0,1:T(8,128)(2,1)} all-gather(bf16[128,64]{0,1:T(8,128)(2,1)S(1)} %fusion.163), channel_id=9, replica_groups=mesh['section'=4,'dp'=32] {'dp'}, dimensions={0}, use_global_device_ids=true | all-gather | bytes 540672 | tf_op jit(solution)/shard_map/all_gather | solution.py:147
  815.0 28.8 %reduce.3 = bf16[5120,128]{1,0:T(8,128)(2,1)S(1)} reduce(bf16[5120,1,128]{2,1,0:T(2,128)(2,1)} %bitcast.617, bf16[]{:T(256)} %broadcast.422), dimensions={1}, to_apply=%bitcast.507.reduce_sub_computation | reduce | bytes 2621442
  845.1 24.1 %all-gather.6 = bf16[4096,64]{0,1:T(8,128)(2,1)S(1)} all-gather(bf16[128,64]{0,1:T(8,128)(2,1)} %fusion.160), channel_id=8, replica_groups=mesh['section'=4,'dp'=32] {'dp'}, dimensions={0}, use_global_device_ids=true | all-gather | bytes 540672 | tf_op jit(solution)/shard_map/all_gather | solution.py:147
  869.2 22.7 %all-gather.5 = bf16[4096,64]{0,1:T(8,128)(2,1)S(1)} all-gather(bf16[128,64]{0,1:T(8,128)(2,1)} %fusion.157), channel_id=7, replica_groups=mesh['section'=4,'dp'=32] {'dp'}, dimensions={0}, use_global_device_ids=true | all-gather | bytes 540672 | tf_op jit(solution)/shard_map/all_gather | solution.py:147
  902.9 37.9 %all-gather.9 = bf16[4096,64]{0,1:T(8,128)(2,1)} all-gather(bf16[128,64]{0,1:T(8,128)(2,1)S(1)} %fusion.169), channel_id=11, replica_groups=mesh['section'=4,'dp'=32] {'dp'}, dimensions={0}, use_global_device_ids=true | all-gather | bytes 540672 | tf_op jit(solution)/shard_map/all_gather | solution.py:147
  946.1 28.8 %reduce.5 = bf16[5120,128]{1,0:T(8,128)(2,1)S(1)} reduce(bf16[5120,1,128]{2,1,0:T(2,128)(2,1)} %bitcast.616, bf16[]{:T(256)} %broadcast.422), dimensions={1}, to_apply=%bitcast.511.reduce_sub_computation | reduce | bytes 2621442
  992.2 7.9 reshape.831
  1015.8 7.7 reshape.833
  1036.1 10.1 fusion.272
  1072.3 7.7 reshape.837
  1082.1 10.0 fusion.269
  1092.1 10.3 fusion.266
  1102.4 10.1 fusion.263
  1125.6 25.5 %all-gather.4 = bf16[4096,64]{0,1:T(8,128)(2,1)S(1)} all-gather(bf16[128,64]{0,1:T(8,128)(2,1)S(1)} %convolution_convert_fusion), channel_id=6, replica_groups=mesh['section'=4,'dp'=32] {'dp'}, dimensions={0}, use_global_device_ids=true | all-gather | bytes 540672 | tf_op jit(solution)/shard_map/all_gather | solution.py:148
  1159.9 13.5 %add_bitcast_fusion = f32[1,128,160,64]{1,2,3,0:T(8,128)S(1)} fusion(f32[128,160,64]{0,1,2:T(8,128)} %fusion.263, f32[128,160,64]{0,1,2:T(8,128)} %fusion.266, f32[128,160,64]{0,1,2:T(8,128)} %fusion.272, f32[128,160,64]{0,1,2:T(8,128)} %fusion.269, f32[160,64,32]{0,2,1:T(8,128)} %copy.109, s32[32]{0:T(128)S(1)} %get-tuple-element.25, pred[]{:T(512)S(6)} %and.40), kind=kOutput, calls=%fused_computation.57 | convolution fusion | flops 508571648 | bytes 27525248 | tf_op jit(solution)/shard_map/dot_general | solution.py:161
  (373 shorter events, 508.2 us)
Async XLA Ops:
  5.2 58.1 %all-to-all-start.1 = ((bf16[32,2,512]{2,1,0:T(2,128)(2,1)}), bf16[32,2,512]{2,1,0:T(2,128)(2,1)S(1)}, u32[]{:S(2)}, u32[]{:S(2)}) async-start(bf16[32,2,512]{2,1,0:T(2,128)(2,1)} %reshape.818), calls=%async_computation.1 | async-start | bytes 131072 | tf_op jit(solution)/shard_map/all_to_all | solution.py:114
  43.1 73.9 %copy-start.29 = (bf16[128,512]{1,0:T(8,128)(2,1)}, bf16[128,512]{1,0:T(8,128)(2,1)S(1)}, u32[]{:S(2)}) copy-start(bf16[128,512]{1,0:T(8,128)(2,1)S(1)} %fusion.140) | copy-start | bytes 393220
  63.3 14.7 %all-to-all-start.3 = ((bf16[32,2,512]{2,1,0:T(2,128)(2,1)}), bf16[32,2,512]{2,1,0:T(2,128)(2,1)S(1)}, u32[]{:S(2)}, u32[]{:S(2)}) async-start(bf16[32,2,512]{2,1,0:T(2,128)(2,1)} %reshape.820), calls=%async_computation.3 | async-start | bytes 131072 | tf_op jit(solution)/shard_map/all_to_all | solution.py:114
  78.1 11.3 all-to-all-start.5
  89.4 11.3 all-to-all-start.9
  100.7 11.3 all-to-all-start.7
  112.1 22.0 %all-to-all-start = ((bf16[32,160,64]{1,2,0:T(8,128)(2,1)}), bf16[32,160,64]{1,2,0:T(8,128)(2,1)}, u32[]{:S(2)}, u32[]{:S(2)}) async-start(bf16[32,160,64]{1,2,0:T(8,128)(2,1)} %gather_fusion.1), calls=%async_computation | async-start | bytes 2097152 | tf_op jit(solution)/shard_map/all_to_all | solution.py:113
  134.0 22.2 %all-to-all-start.2 = ((bf16[32,160,64]{1,2,0:T(8,128)(2,1)}), bf16[32,160,64]{1,2,0:T(8,128)(2,1)}, u32[]{:S(2)}, u32[]{:S(2)}) async-start(bf16[32,160,64]{1,2,0:T(8,128)(2,1)} %gather_fusion.3), calls=%async_computation.2 | async-start | bytes 2097152 | tf_op jit(solution)/shard_map/all_to_all | solution.py:113
  156.2 24.7 %all-to-all-start.4 = ((bf16[32,160,64]{1,2,0:T(8,128)(2,1)}), bf16[32,160,64]{1,2,0:T(8,128)(2,1)}, u32[]{:S(2)}, u32[]{:S(2)}) async-start(bf16[32,160,64]{1,2,0:T(8,128)(2,1)} %gather_fusion.5), calls=%async_computation.4 | async-start | bytes 2097152 | tf_op jit(solution)/shard_map/all_to_all | solution.py:113
  166.4 30.5 %collective-permute-start = (bf16[128,5120]{1,0:T(8,128)(2,1)}, bf16[128,5120]{1,0:T(8,128)(2,1)}, u32[]{:S(2)}, u32[]{:S(2)}) collective-permute-start(bf16[128,5120]{1,0:T(8,128)(2,1)} %fusion.4), channel_id=1, source_target_pairs={{0,32},{32,64},{64,96},{1,33},{33,65},{65,97},{2,34},{34,66},{66,9... | collective-permute-start | bytes 3932168 | tf_op jit(solution)/shard_map/ppermute | solution.py:12
  180.9 34.6 %all-to-all-start.11 = ((bf16[32,160,64]{1,2,0:T(8,128)(2,1)}), bf16[32,160,64]{1,2,0:T(8,128)(2,1)}, u32[]{:S(2)}, u32[]{:S(2)}) async-start(bf16[32,160,64]{1,2,0:T(8,128)(2,1)} %gather_fusion.10), calls=%async_computation.11 | async-start | bytes 2097152 | tf_op jit(solution)/shard_map/all_to_all | solution.py:113
  210.4 39.3 %collective-permute-start.1 = (bf16[128,5120]{1,0:T(8,128)(2,1)}, bf16[128,5120]{1,0:T(8,128)(2,1)}, u32[]{:S(2)}, u32[]{:S(2)}) collective-permute-start(bf16[128,5120]{1,0:T(8,128)(2,1)} %fusion.5), channel_id=1, source_target_pairs={{0,32},{32,64},{64,96},{1,33},{33,65},{65,97},{2,34},{34,66},{66,9... | collective-permute-start | bytes 3932168 | tf_op jit(solution)/shard_map/ppermute | solution.py:12
  215.4 26.0 %all-to-all-start.6 = ((bf16[32,160,64]{1,2,0:T(8,128)(2,1)}), bf16[32,160,64]{1,2,0:T(8,128)(2,1)}, u32[]{:S(2)}, u32[]{:S(2)}) async-start(bf16[32,160,64]{1,2,0:T(8,128)(2,1)} %gather_fusion.7), calls=%async_computation.6 | async-start | bytes 2097152 | tf_op jit(solution)/shard_map/all_to_all | solution.py:113
  263.3 30.5 %collective-permute-start.2 = (bf16[128,5120]{1,0:T(8,128)(2,1)}, bf16[128,5120]{1,0:T(8,128)(2,1)}, u32[]{:S(2)}, u32[]{:S(2)}) collective-permute-start(bf16[128,5120]{1,0:T(8,128)(2,1)} %fusion.6), channel_id=1, source_target_pairs={{0,32},{32,64},{64,96},{1,33},{33,65},{65,97},{2,34},{34,66},{66,9... | collective-permute-start | bytes 3932168 | tf_op jit(solution)/shard_map/ppermute | solution.py:12
  305.3 32.7 %collective-permute-start.3 = (bf16[128,5120]{1,0:T(8,128)(2,1)}, bf16[128,5120]{1,0:T(8,128)(2,1)S(1)}, u32[]{:S(2)}, u32[]{:S(2)}) collective-permute-start(bf16[128,5120]{1,0:T(8,128)(2,1)} %fusion.7), channel_id=1, source_target_pairs={{0,32},{32,64},{64,96},{1,33},{33,65},{65,97},{2,34},{34,66},{66,9... | collective-permute-start | bytes 3932168 | tf_op jit(solution)/shard_map/ppermute | solution.py:12
  338.7 126.9 %copy-start.2 = (bf16[2,128,5120]{2,1,0:T(8,128)(2,1)}, bf16[2,128,5120]{2,1,0:T(8,128)(2,1)S(1)}, u32[]{:S(2)}) copy-start(bf16[2,128,5120]{2,1,0:T(8,128)(2,1)S(1)} %fusion.114) | copy-start | bytes 7864324
  343.9 31.1 %collective-permute-start.4 = (bf16[128,5120]{1,0:T(8,128)(2,1)S(1)}, bf16[128,5120]{1,0:T(8,128)(2,1)S(1)}, u32[]{:S(2)}, u32[]{:S(2)}) collective-permute-start(bf16[128,5120]{1,0:T(8,128)(2,1)S(1)} %fusion.56), channel_id=1, source_target_pairs={{32,0},{64,32},{96,64},{33,1},{65,33},{97,65},{34,2},{66,34},{98,6... | collective-permute-start | bytes 3932168 | tf_op jit(solution)/shard_map/ppermute | solution.py:12
  382.0 29.4 %collective-permute-start.5 = (bf16[128,5120]{1,0:T(8,128)(2,1)S(1)}, bf16[128,5120]{1,0:T(8,128)(2,1)S(1)}, u32[]{:S(2)}, u32[]{:S(2)}) collective-permute-start(bf16[128,5120]{1,0:T(8,128)(2,1)S(1)} %fusion.65), channel_id=1, source_target_pairs={{32,0},{64,32},{96,64},{33,1},{65,33},{97,65},{34,2},{66,34},{98,6... | collective-permute-start | bytes 3932168 | tf_op jit(solution)/shard_map/ppermute | solution.py:12
  419.5 115.8 %collective-permute-start.6 = (bf16[128,5120]{1,0:T(8,128)(2,1)}, bf16[128,5120]{1,0:T(8,128)(2,1)}, u32[]{:S(2)}, u32[]{:S(2)}) collective-permute-start(bf16[128,5120]{1,0:T(8,128)(2,1)} %fusion.74), channel_id=1, source_target_pairs={{32,0},{64,32},{96,64},{33,1},{65,33},{97,65},{34,2},{66,34},{98,6... | collective-permute-start | bytes 3932168 | tf_op jit(solution)/shard_map/ppermute | solution.py:12
  425.2 38.3 %all-to-all-start.15 = ((bf16[32,2,1024]{2,1,0:T(2,128)(2,1)}), bf16[32,2,1024]{2,1,0:T(2,128)(2,1)}, u32[]{:S(2)}, u32[]{:S(2)}) async-start(bf16[32,2,1024]{2,1,0:T(2,128)(2,1)} %reshape.838), calls=%async_computation.15 | async-start | bytes 262144 | tf_op jit(solution)/shard_map/all_to_all | solution.py:144
  468.2 32.8 %all-to-all-start.16 = ((bf16[32,2,1024]{2,1,0:T(2,128)(2,1)}), bf16[32,2,1024]{2,1,0:T(2,128)(2,1)S(1)}, u32[]{:S(2)}, u32[]{:S(2)}) async-start(bf16[32,2,1024]{2,1,0:T(2,128)(2,1)} %reshape.840), calls=%async_computation.16 | async-start | bytes 262144 | tf_op jit(solution)/shard_map/all_to_all | solution.py:144
  473.3 67.5 %slice-start.4 = ((s8[5242880]{0:T(1024)(128)(4,1)}), s8[1048576]{0:T(1024)(128)(4,1)S(1)}, s32[]{:S(2)}) async-start(s8[5242880]{0:T(1024)(128)(4,1)} %bitcast.605), calls=%async_computation.24 | async-start | bytes 2097152
  504.0 30.4 %all-to-all-start.17 = ((bf16[32,2,1024]{2,1,0:T(2,128)(2,1)}), bf16[32,2,1024]{2,1,0:T(2,128)(2,1)S(1)}, u32[]{:S(2)}, u32[]{:S(2)}) async-start(bf16[32,2,1024]{2,1,0:T(2,128)(2,1)} %reshape.842), calls=%async_computation.17 | async-start | bytes 262144 | tf_op jit(solution)/shard_map/all_to_all | solution.py:144
  546.3 54.1 %all-to-all-start.18 = ((bf16[32,2,1024]{2,1,0:T(2,128)(2,1)}), bf16[32,2,1024]{2,1,0:T(2,128)(2,1)}, u32[]{:S(2)}, u32[]{:S(2)}) async-start(bf16[32,2,1024]{2,1,0:T(2,128)(2,1)} %reshape.844), calls=%async_computation.18 | async-start | bytes 262144 | tf_op jit(solution)/shard_map/all_to_all | solution.py:144
  600.4 88.2 %all-to-all-start.13 = ((bf16[32,2,10240]{2,1,0:T(2,128)(2,1)}), bf16[32,2,10240]{2,1,0:T(2,128)(2,1)}, u32[]{:S(2)}, u32[]{:S(2)}) async-start(bf16[32,2,10240]{2,1,0:T(2,128)(2,1)} %reshape.828), calls=%async_computation.13 | async-start | bytes 2621440 | tf_op jit(solution)/shard_map/all_to_all | solution.py:143
  612.6 499.9 %collective-permute-start.7 = (bf16[128,5120]{1,0:T(8,128)(2,1)}, bf16[128,5120]{1,0:T(8,128)(2,1)}, u32[]{:S(2)}, u32[]{:S(2)}) collective-permute-start(bf16[128,5120]{1,0:T(8,128)(2,1)} %fusion.83), channel_id=1, source_target_pairs={{32,0},{64,32},{96,64},{33,1},{65,33},{97,65},{34,2},{66,34},{98,6... | collective-permute-start | bytes 3932168 | tf_op jit(solution)/shard_map/ppermute | solution.py:12
  688.6 79.8 %all-to-all-start.12 = ((bf16[32,2,10240]{2,1,0:T(2,128)(2,1)}), bf16[32,2,10240]{2,1,0:T(2,128)(2,1)}, u32[]{:S(2)}, u32[]{:S(2)}) async-start(bf16[32,2,10240]{2,1,0:T(2,128)(2,1)} %reshape.830), calls=%async_computation.12 | async-start | bytes 2621440 | tf_op jit(solution)/shard_map/all_to_all | solution.py:143
  696.0 68.4 %copy-start.13 = (bf16[1,128,5120]{2,1,0:T(8,128)(2,1)S(1)}, bf16[1,128,5120]{2,1,0:T(8,128)(2,1)}, u32[]{:S(2)}) copy-start(bf16[1,128,5120]{2,1,0:T(8,128)(2,1)} %get-tuple-element.23) | copy-start | bytes 3932164
  768.4 129.1 %all-to-all-start.10 = ((bf16[32,2,10240]{2,1,0:T(2,128)(2,1)}), bf16[32,2,10240]{2,1,0:T(2,128)(2,1)}, u32[]{:S(2)}, u32[]{:S(2)}) async-start(bf16[32,2,10240]{2,1,0:T(2,128)(2,1)} %reshape.834), calls=%async_computation.10 | async-start | bytes 2621440 | tf_op jit(solution)/shard_map/all_to_all | solution.py:143
  897.5 112.9 %all-to-all-start.8 = ((bf16[32,2,10240]{2,1,0:T(2,128)(2,1)}), bf16[32,2,10240]{2,1,0:T(2,128)(2,1)}, u32[]{:S(2)}, u32[]{:S(2)}) async-start(bf16[32,2,10240]{2,1,0:T(2,128)(2,1)} %reshape.832), calls=%async_computation.8 | async-start | bytes 2621440 | tf_op jit(solution)/shard_map/all_to_all | solution.py:143
  1010.4 61.9 %all-to-all-start.14 = ((bf16[32,2,10240]{2,1,0:T(2,128)(2,1)}), bf16[32,2,10240]{2,1,0:T(2,128)(2,1)}, u32[]{:S(2)}, u32[]{:S(2)}) async-start(bf16[32,2,10240]{2,1,0:T(2,128)(2,1)} %reshape.836), calls=%async_computation.14 | async-start | bytes 2621440 | tf_op jit(solution)/shard_map/all_to_all | solution.py:143
  1118.2 60.6 %all-to-all-start.19 = ((bf16[32,2,1024]{2,1,0:T(2,128)(2,1)}), bf16[32,2,1024]{2,1,0:T(2,128)(2,1)S(1)}, u32[]{:S(2)}, u32[]{:S(2)}) async-start(bf16[32,2,1024]{2,1,0:T(2,128)(2,1)} %reshape.846), calls=%async_computation.19 | async-start | bytes 262144 | tf_op jit(solution)/shard_map/all_to_all | solution.py:144
  (53 other events, 860.0 us)
where the time goes:
time: 1200 us; the launch traced here: 1180 us
  blocking collectives  293 us (24%)
  local copies, waits for them, and re-layouts  224 us (19%)
  other arithmetic  193 us (16%)
  matrix products  167 us (14%)
  waiting for transfers between devices  156 us (13%)
  starting transfers between devices  147 us (12%)
    unnamed x15, other arithmetic  154 us
    all_gather x5, blocking collectives, on_device(): lax.all_gather(low_rank, 'dp', axis=0, tiled=True)  149 us
    all_gather x5, blocking collectives, on_device(): lax.all_gather(grad_low, 'dp', axis=0, tiled=True)  144 us
    ppermute x8, waiting for transfers between devices, passed_along(): lax.ppermute(value, axis, [(source, source + steps) for source in range(f...  101 us
    unnamed x158, local copies, waits for them, and re-layouts  86.5 us
    dot_general x5, matrix products, on_device(): jnp.dot(selector, owner_down.reshape(block_total, -1), precision=lax.Prec...  54 us
    all_to_all x5, starting transfers between devices, on_device(): lax.all_to_all(grad_groups, 'dp', split_axis=2, concat_axis=0, tiled=True)  33.3 us
    all_to_all x5, starting transfers between devices, on_device(): lax.all_to_all(down_table[picked], 'dp', split_axis=0, concat_axis=1, til...  31.2 us
  transfers between devices with their start and end apart: 28, of which 11 were waited for; matrix products, arithmetic and copies ran while one was open for 43% of the time, Pallas kernels for 0%

commit v1 on v0

v1 whole, which is shorter than its diff:
```python
import jax
import jax.numpy as jnp
from jax import lax
from jax.experimental import pallas as pl
from jax.experimental.pallas import tpu as pltpu
from jax.sharding import PartitionSpec as P

EPSILON = 1e-06
CHUNK = 32
TILE = 512
GROUP = 16
LANES = 128
BF16 = jnp.bfloat16
F32 = jnp.float32


def dot(left, right):
    return jnp.dot(left, right, preferred_element_type=F32)


def dot_nt(left, right):
    return lax.dot_general(left, right, (((1,), (1,)), ((), ())), preferred_element_type=F32)


def dot_tn(left, right):
    return lax.dot_general(left, right, (((0,), (0,)), ((), ())), preferred_element_type=F32)


def swap_halves(value):
    half = value.shape[-1] // 2
    return jnp.concatenate([value[:, half:], value[:, :half]], axis=1)


def fill_picks(picks, criterion, slot_of):
    micro, blocks = criterion.shape
    lanes = lax.broadcasted_iota(jnp.int32, (1, picks.shape[1]), 1)
    for index in range(micro * blocks):
        slot = slot_of[criterion[index // blocks, index % blocks]]
        picks[index : index + 1, :] = jnp.where(lanes == slot, 1.0, 0.0)


def chain_kernel(
    tokens,
    cotangent,
    gains,
    w_value,
    w_out,
    down,
    up,
    criterion,
    slot_of,
    grad_recv,
    value_ref,
    out_ref,
    down_ref,
    up_ref,
    picks,
    h_in,
    h_out,
    g_in,
    g_out,
    normed,
    inverse,
    value_grad,
    low,
    low_grad,
    scaled,
    panel_send,
    panel_recv,
    panel_down,
    panel_up,
    product_down,
    product_up,
    grad_send,
    load_sem,
    h_send_sem,
    h_recv_sem,
    g_send_sem,
    g_recv_sem,
    panel_send_sem,
    panel_recv_sem,
    grad_send_sem,
    grad_recv_sem,
):
    sections = lax.axis_size("section")
    peers = lax.axis_size("dp")
    section = lax.axis_index("section")
    me = lax.axis_index("dp")
    micro = criterion.shape[0]
    rows, width = h_in.shape
    block = rows // micro
    chunks = rows // CHUNK
    per_block = block // CHUNK
    slots = picks.shape[1]
    feature_rows = down.shape[0]
    value_rows = up.shape[0]
    down_half = feature_rows // 2
    up_half = value_rows // 2
    packed = panel_send.shape[2]
    tiles = [slice(start, start + TILE) for start in range(0, width, TILE)]
    first = section == 0
    last = section == sections - 1

    loads = [
        pltpu.make_async_copy(source, target, load_sem.at[place])
        for place, (source, target) in enumerate(
            [(down, down_ref), (up, up_ref), (w_value, value_ref), (w_out, out_ref)]
        )
    ]
    for load in loads:
        load.start()

    def chunk_rows(c):
        return pl.ds(pl.multiple_of(c * CHUNK, CHUNK), CHUNK)

    @pl.when(first)
    def _():
        for c in range(chunks):
            part = pl.ds(c * CHUNK, CHUNK)
            pltpu.make_async_copy(tokens.at[part], h_in.at[part], h_recv_sem.at[c]).start()

    @pl.when(last)
    def _():
        for c in range(chunks):
            part = pl.ds(c * CHUNK, CHUNK)
            pltpu.make_async_copy(cotangent.at[part], g_in.at[part], g_recv_sem.at[c]).start()

    barrier = pltpu.get_barrier_semaphore()

    def greet(k, carry):
        pl.semaphore_signal(
            barrier,
            inc=1,
            device_id={"dp": lax.rem(me + k, peers)},
            device_id_type=pl.DeviceIdType.MESH,
        )
        return carry

    lax.fori_loop(1, peers, greet, 0)
    for step in (1, sections - 1):
        pl.semaphore_signal(
            barrier,
            inc=1,
            device_id={"section": lax.rem(section + step, sections)},
            device_id_type=pl.DeviceIdType.MESH,
        )

    fill_picks(picks, criterion, slot_of)
    chosen = picks[...].astype(BF16)
    loads[0].wait()
    loads[1].wait()
    for start in range(0, down_half, GROUP):
        pair = jnp.concatenate(
            [down_ref[start : start + GROUP], down_ref[down_half + start : down_half + start + GROUP]],
            axis=1,
        )
        found = dot_nt(chosen, pair.reshape(GROUP * LANES, slots))
        found = found.reshape(micro, peers, GROUP, LANES).astype(BF16)
        panel_send[:, :, start : start + GROUP, :] = found
    pair = jnp.concatenate([up_ref[0:up_half], up_ref[up_half:value_rows]], axis=1)
    found = dot_nt(chosen, pair.reshape(up_half * LANES, slots)).reshape(
        micro, peers, up_half, LANES
    )
    if packed - down_half > up_half:
        rest = jnp.zeros((micro, peers, packed - down_half - up_half, LANES), F32)
        found = jnp.concatenate([found, rest], axis=2)
    panel_send[:, :, down_half:packed, :] = found.astype(BF16)

    pl.semaphore_wait(barrier, peers + 1)

    def spread(m, source, target, send_sem, recv_sem):
        def send(k, carry):
            peer = lax.rem(me + k, peers)
            pltpu.make_async_remote_copy(
                src_ref=source.at[m, peer],
                dst_ref=target.at[m, me],
                send_sem=send_sem.at[m],
                recv_sem=recv_sem.at[m],
                device_id={"dp": peer},
                device_id_type=pl.DeviceIdType.MESH,
            ).start()
            return carry

        pltpu.make_async_copy(source.at[m, me], target.at[m, me], recv_sem.at[m]).start()
        lax.fori_loop(1, peers, send, 0)

    def wait_for(ref, sem):
        pltpu.make_async_copy(ref, ref, sem).wait()

    for m in range(micro):
        spread(m, panel_send, panel_recv, panel_send_sem, panel_recv_sem)

    loads[2].wait()
    loads[3].wait()

    lane = lax.broadcasted_iota(jnp.int32, (CHUNK, LANES), 1)
    own_lanes = lane < LANES // 2

    def unpack(m):
        wait_for(panel_recv.at[m], panel_recv_sem.at[m])

        def one(source, carry):
            at = pl.multiple_of(source * feature_rows, 2 * GROUP)
            part = panel_recv[m, source, 0:down_half, :]
            panel_down[m, pl.ds(at, down_half), :] = part
            panel_down[m, pl.ds(at + down_half, down_half), :] = swap_halves(part)
            at = pl.multiple_of(source * value_rows, GROUP)
            part = panel_recv[m, source, down_half:packed, :].astype(F32)[0:up_half]
            both = jnp.concatenate([part, swap_halves(part)], axis=0)
            panel_up[m, pl.ds(at, value_rows), :] = both.astype(BF16)
            return carry

        lax.fori_loop(0, peers, one, 0)

    def forward(c):
        m = c // per_block
        here = chunk_rows(c)
        wait_for(h_in.at[here], h_recv_sem.at[c])
        total = jnp.zeros((CHUNK, 1), F32)
        for tile in tiles:
            hidden = h_in[here, tile].astype(F32)
            total += jnp.sum(hidden * hidden, axis=1, keepdims=True)
        factor = lax.rsqrt(total / width + EPSILON)
        inverse[here, :] = jnp.broadcast_to(factor, (CHUNK, LANES))
        mixed = jnp.zeros((CHUNK, w_value.shape[1]), F32)
        for tile in tiles:
            hidden = h_in[here, tile].astype(F32)
            part = (hidden * factor * gains[:, tile]).astype(BF16)
            normed[here, tile] = part
            mixed += dot(part, value_ref[tile, :])

        @pl.when(c % per_block == 0)
        def _():
            unpack(m)

        narrow = jnp.zeros((CHUNK, LANES), F32)
        for tile in tiles:
            narrow += dot(normed[here, tile], panel_down[m, tile, :])
        narrow = jnp.where(own_lanes, narrow, 0.0).astype(BF16)
        low[here, :] = narrow

        @pl.when(section < sections - 1)
        def _():
            values = (mixed + dot_nt(narrow, panel_up[m])).astype(BF16)
            for tile in tiles:
                added = dot(values, out_ref[:, tile])
                h_out[here, tile] = (h_in[here, tile].astype(F32) + added).astype(BF16)
            pltpu.make_async_remote_copy(
                src_ref=h_out.at[here],
                dst_ref=h_in.at[here],
                send_sem=h_send_sem.at[c],
                recv_sem=h_recv_sem.at[c],
                device_id={"section": section + 1},
                device_id_type=pl.DeviceIdType.MESH,
            ).start()

    def backward(c):
        m = c // per_block
        here = chunk_rows(c)
        wait_for(g_in.at[here], g_recv_sem.at[c])
        pulled = jnp.zeros((CHUNK, w_value.shape[1]), F32)
        for tile in tiles:
            pulled += dot_nt(g_in[here, tile], out_ref[:, tile])
        pulled = pulled.astype(BF16)
        value_grad[here, :] = pulled
        narrow = jnp.where(own_lanes, dot(pulled, panel_up[m]), 0.0).astype(BF16)
        low_grad[here, :] = narrow

        @pl.when(section > 0)
        def _():
            moment = jnp.zeros((CHUNK, 1), F32)
            for tile in tiles:
                part = dot_nt(pulled, value_ref[tile, :]) + dot_nt(narrow, panel_down[m, tile, :])
                part = part * gains[:, tile]
                scaled[:, tile] = part
                moment += jnp.sum(part * h_in[here, tile].astype(F32), axis=1, keepdims=True)
            factor = inverse[here, 0:1]
            bend = factor * factor * factor * (moment / width)
            for tile in tiles:
                result = (
                    g_in[here, tile].astype(F32)
                    + factor * scaled[:, tile]
                    - h_in[here, tile].astype(F32) * bend
                )
                g_out[here, tile] = result.astype(BF16)
            pltpu.make_async_remote_copy(
                src_ref=g_out.at[here],
                dst_ref=g_in.at[here],
                send_sem=g_send_sem.at[c],
                recv_sem=g_recv_sem.at[c],
                device_id={"section": section - 1},
                device_id_type=pl.DeviceIdType.MESH,
            ).start()

    def products(m):
        here = pl.ds(pl.multiple_of(m * block, block), block)
        for tile in tiles:
            product_down[tile, :] = dot_tn(normed[here, tile], low_grad[here, :]).astype(BF16)
        product_up[...] = dot_tn(value_grad[here, :], low[here, :])

        def pack(peer, carry):
            at = pl.multiple_of(peer * feature_rows, 2 * GROUP)
            part = product_down[pl.ds(at, down_half), :]
            other = product_down[pl.ds(at + down_half, down_half), :]
            grad_send[m, peer, 0:down_half, :] = part + swap_halves(other)
            at = pl.multiple_of(peer * value_rows, GROUP)
            part = product_up[pl.ds(at, value_rows), :]
            part = part[0:up_half] + swap_halves(part[up_half:value_rows])
            if packed - down_half > up_half:
                rest = jnp.zeros((packed - down_half - up_half, LANES), F32)
                part = jnp.concatenate([part, rest], axis=0)
            grad_send[m, peer, down_half:packed, :] = part.astype(BF16)
            return carry

        lax.fori_loop(0, peers, pack, 0)
        spread(m, grad_send, grad_recv, grad_send_sem, grad_recv_sem)

    lag = jnp.where(first, chunks, jnp.where(last, 0, (sections - 1 - section) * 3))
    lag = jnp.minimum(lag, chunks)

    def step(t, carry):
        @pl.when(t < chunks)
        def _():
            forward(t)

        c = t - lag

        @pl.when((c >= 0) & (c < chunks))
        def _():
            backward(c)

            @pl.when(c % per_block == per_block - 1)
            def _():
                products(c // per_block)

        return carry

    lax.fori_loop(0, chunks + lag, step, 0)

    for m in range(micro):
        wait_for(grad_recv.at[m], grad_recv_sem.at[m])
        for source, sem in ((panel_send, panel_send_sem), (grad_send, grad_send_sem)):
            wait_for(source.at[m, 0 : peers - 1], sem.at[m])

    @pl.when(section < sections - 1)
    def _():
        for c in range(chunks):
            wait_for(h_out.at[pl.ds(c * CHUNK, CHUNK)], h_send_sem.at[c])

    @pl.when(section > 0)
    def _():
        for c in range(chunks):
            wait_for(g_out.at[pl.ds(c * CHUNK, CHUNK)], g_send_sem.at[c])


def run_chain(tokens, cotangent, gains, w_value, w_out, down, up, criterion, slot_of):
    micro = criterion.shape[0]
    peers = lax.axis_size("dp")
    rows, width = tokens.shape
    value_width = w_out.shape[0]
    chunks = rows // CHUNK
    slots = down.shape[2]
    useful = (down.shape[0] + up.shape[0]) // 2
    packed = (useful + 15) // 16 * 16
    block = rows // micro
    spaces = [pl.BlockSpec(memory_space=pl.ANY)] * 2
    spaces += [pl.BlockSpec(memory_space=pltpu.VMEM)]
    spaces += [pl.BlockSpec(memory_space=pl.ANY)] * 4
    spaces += [pl.BlockSpec(memory_space=pltpu.SMEM)] * 2
    row_buffer = pltpu.VMEM((rows, width), BF16)
    exchange = (micro, peers, packed, LANES)
    return pl.pallas_call(
        chain_kernel,
        out_shape=jax.ShapeDtypeStruct(exchange, BF16),
        in_specs=spaces,
        out_specs=pl.BlockSpec(memory_space=pl.ANY),
        scratch_shapes=[
            pltpu.VMEM(w_value.shape, BF16),
            pltpu.VMEM(w_out.shape, BF16),
            pltpu.VMEM(down.shape, BF16),
            pltpu.VMEM(up.shape, BF16),
            pltpu.VMEM((micro * criterion.shape[1], slots), F32),
            row_buffer,
            row_buffer,
            row_buffer,
            row_buffer,
            row_buffer,
            pltpu.VMEM((rows, LANES), F32),
            pltpu.VMEM((rows, value_width), BF16),
            pltpu.VMEM((rows, LANES), BF16),
            pltpu.VMEM((rows, LANES), BF16),
            pltpu.VMEM((CHUNK, width), F32),
            pltpu.VMEM(exchange, BF16),
            pltpu.VMEM(exchange, BF16),
            pltpu.VMEM((micro, width, LANES), BF16),
            pltpu.VMEM((micro, value_width, LANES), BF16),
            pltpu.VMEM((width, LANES), BF16),
            pltpu.VMEM((value_width, LANES), F32),
            pltpu.VMEM(exchange, BF16),
            pltpu.SemaphoreType.DMA((4,)),
            pltpu.SemaphoreType.DMA((chunks,)),
            pltpu.SemaphoreType.DMA((chunks,)),
            pltpu.SemaphoreType.DMA((chunks,)),
            pltpu.SemaphoreType.DMA((chunks,)),
            pltpu.SemaphoreType.DMA((micro,)),
            pltpu.SemaphoreType.DMA((micro,)),
            pltpu.SemaphoreType.DMA((micro,)),
            pltpu.SemaphoreType.DMA((micro,)),
        ],
        compiler_params=pltpu.CompilerParams(
            collective_id=0, has_side_effects=True, vmem_limit_bytes=56 * 1024 * 1024
        ),
        name="chain",
    )(tokens, cotangent, gains, w_value, w_out, down, up, criterion, slot_of)


def place_kernel(criterion, slot_of, parts, down, up, picks):
    step = pl.program_id(0)
    pairs = parts.shape[0]
    up_half = up.shape[0] // 2

    @pl.when(step == 0)
    def _():
        fill_picks(picks, criterion, slot_of)

    chosen = picks[...].astype(BF16)
    flat = parts[...].reshape(pairs, GROUP * LANES)
    summed = dot_tn(flat, chosen).reshape(GROUP, 2, LANES // 2, picks.shape[1])

    @pl.when(step < pl.num_programs(0) - 1)
    def _():
        down[0] = summed[:, 0]
        down[1] = summed[:, 1]

    @pl.when(step == pl.num_programs(0) - 1)
    def _():
        up[0:up_half] = summed[0:up_half, 0]
        up[up_half : 2 * up_half] = summed[0:up_half, 1]


def place(criterion, slot_of, parts, feature_rows, value_rows, slots, rank):
    pairs = parts.shape[0]
    down_half = feature_rows // 2
    steps = down_half // GROUP
    down, up = pl.pallas_call(
        place_kernel,
        grid=(steps + 1,),
        in_specs=[
            pl.BlockSpec(memory_space=pltpu.SMEM),
            pl.BlockSpec(memory_space=pltpu.SMEM),
            pl.BlockSpec((pairs, GROUP, LANES), lambda i: (0, i, 0)),
        ],
        out_specs=[
            pl.BlockSpec((2, GROUP, rank, slots), lambda i: (0, jnp.minimum(i, steps - 1), 0, 0)),
            pl.BlockSpec((value_rows, rank, slots), lambda i: (0, 0, 0)),
        ],
        out_shape=[
            jax.ShapeDtypeStruct((2, down_half, rank, slots), F32),
            jax.ShapeDtypeStruct((value_rows, rank, slots), F32),
        ],
        scratch_shapes=[pltpu.VMEM((pairs, slots), F32)],
        compiler_params=pltpu.CompilerParams(vmem_limit_bytes=32 * 1024 * 1024),
        name="place",
    )(criterion, slot_of, parts)
    return down.reshape(feature_rows, rank, slots), up


def on_device(
    tokens,
    cotangent,
    norm_gain,
    value_weight,
    out_weight,
    adapter_down,
    adapter_up,
    criterion,
    slot_of,
):
    micro, block, width = tokens.shape
    down = jnp.transpose(adapter_down[0], (1, 2, 0))
    up = jnp.transpose(adapter_up[0], (1, 2, 0))
    parts = run_chain(
        tokens.reshape(micro * block, width),
        cotangent.reshape(micro * block, width),
        norm_gain,
        value_weight[0],
        out_weight[0],
        down,
        up,
        criterion,
        slot_of,
    )
    parts = parts.reshape((parts.shape[0] * parts.shape[1],) + parts.shape[2:])
    grad_down, grad_up = place(
        criterion, slot_of, parts, down.shape[0], up.shape[0], down.shape[2], down.shape[1]
    )
    return (jnp.transpose(grad_down, (2, 0, 1))[None], jnp.transpose(grad_up, (2, 0, 1))[None])


def solution(mesh):
    return jax.shard_map(
        on_device,
        mesh=mesh,
        in_specs=(
            P(None, "dp", None),
            P(None, "dp", None),
            P("section", None),
            P("section", None, None),
            P("section", None, None),
            P("section", None, "dp", None),
            P("section", None, "dp", None),
            P(),
            P(),
        ),
        out_specs=(P("section", None, "dp", None), P("section", None, "dp", None)),
        check_vma=False,
    )
```

time: 1200 us -> 179 us (0.15); the launches traced: 1180 us -> 179 us
  blocking collectives: 293 us -> 0 us
  local copies, waits for them, and re-layouts: 224 us -> 1.41 us
  other arithmetic: 193 us -> 0 us
  Pallas kernels: 0 us -> 177 us
  matrix products: 167 us -> 0 us
  waiting for transfers between devices: 156 us -> 0 us
  starting transfers between devices: 147 us -> 0 us
    all_gather x10 -> x0, blocking collectives: 293 us -> none  [the longest x5 149 us: on_device(): lax.all_gather(low_rank, 'dp', axis=0, tiled=True)]
    pallas_call x0 -> x2, Pallas kernels: none -> 177 us  [the longest x1 172 us: run_chain(): pl.pallas_call(chain_kernel, out_shape=jax.ShapeDtypeStruct(exchange, BF1...]
    dot_general x52 -> x0, matrix products: 167 us -> none  [the longest x5 54 us: on_device(): jnp.dot(selector, owner_down.reshape(block_total, -1), precision=lax.Prec...]
    unnamed x15 -> x0, other arithmetic: 154 us -> none
    all_to_all x20 -> x0, starting transfers between devices: 123 us -> none  [the longest x5 33.3 us: on_device(): lax.all_to_all(grad_groups, 'dp', split_axis=2, concat_axis=0, tiled=True)]
    ppermute x8 -> x0, waiting for transfers between devices: 101 us -> none  [passed_along(): lax.ppermute(value, axis, [(source, source + steps) for source in range(f...]
    unnamed x158 -> x6, local copies, waits for them, and re-layouts: 86.5 us -> 1.41 us
    all_to_all x20 -> x0, waiting for transfers between devices: 54.4 us -> none  [the longest x5 27.9 us: on_device(): lax.all_to_all(up_table[picked], 'dp', split_axis=0, concat_axis=1, tiled...]
  transfers between devices with their start and end apart: 28 -> 0, of which waited for: 11 -> 0; matrix products, arithmetic and copies ran while one was open for 43% -> 0% of each run, Pallas kernels for 0% -> 0%
where the time goes in v1:
time: 179 us
  Pallas kernels  177 us (99%)
    pallas_call x1, Pallas kernels, run_chain(): pl.pallas_call(chain_kernel, out_shape=jax.ShapeDtypeStruct(exchange, BF1...  172 us
    pallas_call x1, Pallas kernels, place(): pl.pallas_call(place_kernel, grid=(steps + 1,), in_specs=[pl.BlockSpec(me...  5.41 us

profile of v1, /device:TPU:1, one launch (start us, length us, event | category | flops | bytes accessed | tf_op | source)
XLA Modules:
  0.0 179.2 jit_solution(4531750289352603658)
XLA Ops:
  0.6 0.0 copy-start.1
  0.6 0.0 copy-start.2
  0.7 171.7 %chain.1 = bf16[2,32,96,128]{3,2,1,0:T(8,128)(2,1)} custom-call(bf16[256,5120]{1,0:T(8,128)(2,1)} %bitcast.22, bf16[256,5120]{1,0:T(8,128)(2,1)} %bitcast.23, f32[1,5120]{1,0:T(1,128)} %gains.1, bf16[5120,512]{1,0:T(8,128)(2,1)} %bitcast.20, bf16[512,5120]{1,0:T(8,128)(2,1)} %bitcast.21, bf16[160,64,128]{2,1,0:T(8,128)(2,1)} %bitcast.24, ...), custom_call_target="tpu_custom_call" | custom-call | tf_op jit(solution)/shard_map/chain/pallas_call | solution.py:372
  172.4 0.0 copy-done.1
  172.4 0.0 copy-done.2
  172.4 0.0 copy-start
  172.4 1.4 copy-done
  173.8 5.4 %place.1 = (f32[2,80,64,128]{3,2,1,0:T(8,128)}, f32[16,64,128]{2,1,0:T(8,128)}) custom-call(s32[2,32]{1,0:T(2,128)S(1)} %copy-done.1, s32[128]{0:T(128)S(1)} %copy-done.2, bf16[64,96,128]{2,1,0:T(8,128)(2,1)S(1)} %bitcast.19), custom_call_target="tpu_custom_call" | custom-call | tf_op jit(solution)/shard_map/place/pallas_call | solution.py:445
Async XLA Ops:
  0.6 171.8 %copy-start.1 = (s32[2,32]{1,0:T(2,128)S(1)}, s32[2,32]{1,0:T(2,128)}, u32[]{:S(2)}) copy-start(s32[2,32]{1,0:T(2,128)} %criterion.3) | copy-start | bytes 772
  0.6 171.8 %copy-start.2 = (s32[128]{0:T(128)S(1)}, s32[128]{0:T(128)}, u32[]{:S(2)}) copy-start(s32[128]{0:T(128)} %slot_of.3) | copy-start | bytes 1540
  172.4 1.4 copy-start

commit v2 on v1

--- a/solution.py
+++ b/solution.py
@@ -9,6 +9,7 @@
 CHUNK = 32
 TILE = 512
 GROUP = 16
+PIECES = 2
 LANES = 128
 BF16 = jnp.bfloat16
 F32 = jnp.float32
@@ -52,6 +53,8 @@
     grad_recv,
     value_ref,
     out_ref,
+    value_turned,
+    out_turned,
     down_ref,
     up_ref,
     picks,
@@ -59,12 +62,13 @@
     h_out,
     g_in,
     g_out,
-    normed,
+    scaled,
     inverse,
+    mixed_ref,
+    narrow_ref,
     value_grad,
     low,
     low_grad,
-    scaled,
     panel_send,
     panel_recv,
     panel_down,
@@ -97,7 +101,9 @@
     down_half = feature_rows // 2
     up_half = value_rows // 2
     packed = panel_send.shape[2]
-    tiles = [slice(start, start + TILE) for start in range(0, width, TILE)]
+    value_width = value_grad.shape[1]
+    piece_width = width // PIECES
+    pieces = [slice(start, start + piece_width) for start in range(0, width, piece_width)]
     first = section == 0
     last = section == sections - 1
 
@@ -110,6 +116,10 @@
     for load in loads:
         load.start()
 
+    def tiles_of(piece):
+        base = piece * piece_width
+        return [slice(base + at, base + at + TILE) for at in range(0, piece_width, TILE)]
+
     def chunk_rows(c):
         return pl.ds(pl.multiple_of(c * CHUNK, CHUNK), CHUNK)
 
@@ -117,13 +127,23 @@
     def _():
         for c in range(chunks):
             part = pl.ds(c * CHUNK, CHUNK)
-            pltpu.make_async_copy(tokens.at[part], h_in.at[part], h_recv_sem.at[c]).start()
+            for piece in range(PIECES):
+                pltpu.make_async_copy(
+                    tokens.at[part, pieces[piece]],
+                    h_in.at[part, pieces[piece]],
+                    h_recv_sem.at[c, piece],
+                ).start()
 
     @pl.when(last)
     def _():
         for c in range(chunks):
             part = pl.ds(c * CHUNK, CHUNK)
-            pltpu.make_async_copy(cotangent.at[part], g_in.at[part], g_recv_sem.at[c]).start()
+            for piece in range(PIECES):
+                pltpu.make_async_copy(
+                    cotangent.at[part, pieces[piece]],
+                    g_in.at[part, pieces[piece]],
+                    g_recv_sem.at[c, piece],
+                ).start()
 
     barrier = pltpu.get_barrier_semaphore()
 
@@ -193,119 +213,130 @@
     loads[2].wait()
     loads[3].wait()
 
-    lane = lax.broadcasted_iota(jnp.int32, (CHUNK, LANES), 1)
-    own_lanes = lane < LANES // 2
-
     def unpack(m):
         wait_for(panel_recv.at[m], panel_recv_sem.at[m])
+        near = lax.broadcasted_iota(jnp.int32, (down_half, LANES), 1) < LANES // 2
+        near_up = lax.broadcasted_iota(jnp.int32, (up_half, LANES), 1) < LANES // 2
 
         def one(source, carry):
             at = pl.multiple_of(source * feature_rows, 2 * GROUP)
             part = panel_recv[m, source, 0:down_half, :]
-            panel_down[m, pl.ds(at, down_half), :] = part
-            panel_down[m, pl.ds(at + down_half, down_half), :] = swap_halves(part)
+            none = jnp.zeros_like(part)
+            panel_down[m, pl.ds(at, down_half), :] = jnp.where(near, part, none)
+            panel_down[m, pl.ds(at + down_half, down_half), :] = jnp.where(near, none, part)
             at = pl.multiple_of(source * value_rows, GROUP)
             part = panel_recv[m, source, down_half:packed, :].astype(F32)[0:up_half]
-            both = jnp.concatenate([part, swap_halves(part)], axis=0)
-            panel_up[m, pl.ds(at, value_rows), :] = both.astype(BF16)
+            both = [jnp.where(near_up, part, 0.0), jnp.where(near_up, 0.0, part)]
+            panel_up[m, pl.ds(at, value_rows), :] = jnp.concatenate(both, axis=0).astype(BF16)
             return carry
 
         lax.fori_loop(0, peers, one, 0)
+
+    def send_piece(source, target, c, piece, send_sem, recv_sem, to):
+        here = chunk_rows(c)
+        columns = pieces[piece]
+        pltpu.make_async_remote_copy(
+            src_ref=source.at[here, columns],
+            dst_ref=target.at[here, columns],
+            send_sem=send_sem.at[c, piece],
+            recv_sem=recv_sem.at[c, piece],
+            device_id={"section": to},
+            device_id_type=pl.DeviceIdType.MESH,
+        ).start()
 
     def forward(c):
         m = c // per_block
         here = chunk_rows(c)
-        wait_for(h_in.at[here], h_recv_sem.at[c])
-        total = jnp.zeros((CHUNK, 1), F32)
-        for tile in tiles:
-            hidden = h_in[here, tile].astype(F32)
-            total += jnp.sum(hidden * hidden, axis=1, keepdims=True)
+        squares = jnp.zeros((CHUNK, LANES), F32)
+        mixed = jnp.zeros((CHUNK, value_width), F32)
+        for piece in range(PIECES):
+            wait_for(h_in.at[here, pieces[piece]], h_recv_sem.at[c, piece])
+            for tile in tiles_of(piece):
+                hidden = h_in[here, tile].astype(F32)
+                square = hidden * hidden
+                for start in range(0, TILE, LANES):
+                    squares += square[:, start : start + LANES]
+                part = (hidden * gains[:, tile]).astype(BF16)
+                scaled[here, tile] = part
+                mixed += dot(part, value_ref[tile, :])
+        total = jnp.sum(squares, axis=1, keepdims=True)
         factor = lax.rsqrt(total / width + EPSILON)
         inverse[here, :] = jnp.broadcast_to(factor, (CHUNK, LANES))
-        mixed = jnp.zeros((CHUNK, w_value.shape[1]), F32)
-        for tile in tiles:
-            hidden = h_in[here, tile].astype(F32)
-            part = (hidden * factor * gains[:, tile]).astype(BF16)
-            normed[here, tile] = part
-            mixed += dot(part, value_ref[tile, :])
+        mixed_ref[here, :] = mixed
 
         @pl.when(c % per_block == 0)
         def _():
             unpack(m)
 
         narrow = jnp.zeros((CHUNK, LANES), F32)
-        for tile in tiles:
-            narrow += dot(normed[here, tile], panel_down[m, tile, :])
-        narrow = jnp.where(own_lanes, narrow, 0.0).astype(BF16)
+        for piece in range(PIECES):
+            for tile in tiles_of(piece):
+                narrow += dot(scaled[here, tile], panel_down[m, tile, :])
+        narrow_ref[here, :] = narrow
+        narrow = ((narrow + swap_halves(narrow)) * factor).astype(BF16)
         low[here, :] = narrow
 
         @pl.when(section < sections - 1)
         def _():
-            values = (mixed + dot_nt(narrow, panel_up[m])).astype(BF16)
-            for tile in tiles:
-                added = dot(values, out_ref[:, tile])
-                h_out[here, tile] = (h_in[here, tile].astype(F32) + added).astype(BF16)
-            pltpu.make_async_remote_copy(
-                src_ref=h_out.at[here],
-                dst_ref=h_in.at[here],
-                send_sem=h_send_sem.at[c],
-                recv_sem=h_recv_sem.at[c],
-                device_id={"section": section + 1},
-                device_id_type=pl.DeviceIdType.MESH,
-            ).start()
+            values = (mixed * factor + dot_nt(narrow, panel_up[m])).astype(BF16)
+            for piece in range(PIECES):
+                for tile in tiles_of(piece):
+                    added = dot(values, out_ref[:, tile])
+                    h_out[here, tile] = (h_in[here, tile].astype(F32) + added).astype(BF16)
+                send_piece(h_out, h_in, c, piece, h_send_sem, h_recv_sem, section + 1)
 
     def backward(c):
         m = c // per_block
         here = chunk_rows(c)
-        wait_for(g_in.at[here], g_recv_sem.at[c])
-        pulled = jnp.zeros((CHUNK, w_value.shape[1]), F32)
-        for tile in tiles:
-            pulled += dot_nt(g_in[here, tile], out_ref[:, tile])
+        pulled = jnp.zeros((CHUNK, value_width), F32)
+        for piece in range(PIECES):
+            wait_for(g_in.at[here, pieces[piece]], g_recv_sem.at[c, piece])
+            for tile in tiles_of(piece):
+                pulled += dot(g_in[here, tile], out_turned[tile, :])
         pulled = pulled.astype(BF16)
         value_grad[here, :] = pulled
-        narrow = jnp.where(own_lanes, dot(pulled, panel_up[m]), 0.0).astype(BF16)
-        low_grad[here, :] = narrow
+        narrow = dot(pulled, panel_up[m])
+        narrow = narrow + swap_halves(narrow)
+        factor = inverse[here, 0:1]
+        low_grad[here, :] = (narrow * factor).astype(BF16)
 
         @pl.when(section > 0)
         def _():
-            moment = jnp.zeros((CHUNK, 1), F32)
-            for tile in tiles:
-                part = dot_nt(pulled, value_ref[tile, :]) + dot_nt(narrow, panel_down[m, tile, :])
-                part = part * gains[:, tile]
-                scaled[:, tile] = part
-                moment += jnp.sum(part * h_in[here, tile].astype(F32), axis=1, keepdims=True)
-            factor = inverse[here, 0:1]
+            held = narrow.astype(BF16)
+            along = pulled.astype(F32) * mixed_ref[here, :]
+            moment = jnp.sum(along, axis=1, keepdims=True)
+            along = held.astype(F32) * narrow_ref[here, :]
+            moment += jnp.sum(along, axis=1, keepdims=True)
             bend = factor * factor * factor * (moment / width)
-            for tile in tiles:
-                result = (
-                    g_in[here, tile].astype(F32)
-                    + factor * scaled[:, tile]
-                    - h_in[here, tile].astype(F32) * bend
-                )
-                g_out[here, tile] = result.astype(BF16)
-            pltpu.make_async_remote_copy(
-                src_ref=g_out.at[here],
-                dst_ref=g_in.at[here],
-                send_sem=g_send_sem.at[c],
-                recv_sem=g_recv_sem.at[c],
-                device_id={"section": section - 1},
-                device_id_type=pl.DeviceIdType.MESH,
-            ).start()
+            for piece in range(PIECES):
+                for tile in tiles_of(piece):
+                    part = dot(pulled, value_turned[:, tile])
+                    part += dot_nt(held, panel_down[m, tile, :])
+                    result = (
+                        g_in[here, tile].astype(F32)
+                        + factor * (part * gains[:, tile])
+                        - h_in[here, tile].astype(F32) * bend
+                    )
+                    g_out[here, tile] = result.astype(BF16)
+                send_piece(g_out, g_in, c, piece, g_send_sem, g_recv_sem, section - 1)
 
     def products(m):
         here = pl.ds(pl.multiple_of(m * block, block), block)
-        for tile in tiles:
-            product_down[tile, :] = dot_tn(normed[here, tile], low_grad[here, :]).astype(BF16)
+        for start in range(0, width, TILE):
+            tile = slice(start, start + TILE)
+            product_down[tile, :] = dot_tn(scaled[here, tile], low_grad[here, :]).astype(BF16)
         product_up[...] = dot_tn(value_grad[here, :], low[here, :])
+        near = lax.broadcasted_iota(jnp.int32, (down_half, LANES), 1) < LANES // 2
+        near_up = lax.broadcasted_iota(jnp.int32, (up_half, LANES), 1) < LANES // 2
 
         def pack(peer, carry):
             at = pl.multiple_of(peer * feature_rows, 2 * GROUP)
             part = product_down[pl.ds(at, down_half), :]
             other = product_down[pl.ds(at + down_half, down_half), :]
-            grad_send[m, peer, 0:down_half, :] = part + swap_halves(other)
+            grad_send[m, peer, 0:down_half, :] = jnp.where(near, part, other)
             at = pl.multiple_of(peer * value_rows, GROUP)
             part = product_up[pl.ds(at, value_rows), :]
-            part = part[0:up_half] + swap_halves(part[up_half:value_rows])
+            part = jnp.where(near_up, part[0:up_half], part[up_half:value_rows])
             if packed - down_half > up_half:
                 rest = jnp.zeros((packed - down_half - up_half, LANES), F32)
                 part = jnp.concatenate([part, rest], axis=0)
@@ -315,10 +346,25 @@
         lax.fori_loop(0, peers, pack, 0)
         spread(m, grad_send, grad_recv, grad_send_sem, grad_recv_sem)
 
+    def turn():
+        def one(index, carry):
+            at = pl.ds(pl.multiple_of(index * TILE, TILE), TILE)
+            out_turned[at, :] = out_ref[:, at].T
+            value_turned[:, at] = value_ref[at, :].T
+            return carry
+
+        lax.fori_loop(0, width // TILE, one, 0)
+
     lag = jnp.where(first, chunks, jnp.where(last, 0, (sections - 1 - section) * 3))
     lag = jnp.minimum(lag, chunks)
 
+    turn_at = jnp.where(first, chunks, 0)
+
     def step(t, carry):
+        @pl.when(t == turn_at)
+        def _():
+            turn()
+
         @pl.when(t < chunks)
         def _():
             forward(t)
@@ -345,12 +391,16 @@
     @pl.when(section < sections - 1)
     def _():
         for c in range(chunks):
-            wait_for(h_out.at[pl.ds(c * CHUNK, CHUNK)], h_send_sem.at[c])
+            for piece in range(PIECES):
+                part = h_out.at[pl.ds(c * CHUNK, CHUNK), pieces[piece]]
+                wait_for(part, h_send_sem.at[c, piece])
 
     @pl.when(section > 0)
     def _():
         for c in range(chunks):
-            wait_for(g_out.at[pl.ds(c * CHUNK, CHUNK)], g_send_sem.at[c])
+            for piece in range(PIECES):
+                part = g_out.at[pl.ds(c * CHUNK, CHUNK), pieces[piece]]
+                wait_for(part, g_send_sem.at[c, piece])
 
 
 def run_chain(tokens, cotangent, gains, w_value, w_out, down, up, criterion, slot_of):
@@ -377,6 +427,8 @@
         scratch_shapes=[
             pltpu.VMEM(w_value.shape, BF16),
             pltpu.VMEM(w_out.shape, BF16),
+            pltpu.VMEM(w_out.shape, BF16),
+            pltpu.VMEM(w_value.shape, BF16),
             pltpu.VMEM(down.shape, BF16),
             pltpu.VMEM(up.shape, BF16),
             pltpu.VMEM((micro * criterion.shape[1], slots), F32),
@@ -386,10 +438,11 @@
             row_buffer,
             row_buffer,
             pltpu.VMEM((rows, LANES), F32),
+            pltpu.VMEM((rows, value_width), F32),
+            pltpu.VMEM((rows, LANES), F32),
             pltpu.VMEM((rows, value_width), BF16),
             pltpu.VMEM((rows, LANES), BF16),
             pltpu.VMEM((rows, LANES), BF16),
-            pltpu.VMEM((CHUNK, width), F32),
             pltpu.VMEM(exchange, BF16),
             pltpu.VMEM(exchange, BF16),
             pltpu.VMEM((micro, width, LANES), BF16),
@@ -398,10 +451,10 @@
             pltpu.VMEM((value_width, LANES), F32),
             pltpu.VMEM(exchange, BF16),
             pltpu.SemaphoreType.DMA((4,)),
-            pltpu.SemaphoreType.DMA((chunks,)),
-            pltpu.SemaphoreType.DMA((chunks,)),
-            pltpu.SemaphoreType.DMA((chunks,)),
-            pltpu.SemaphoreType.DMA((chunks,)),
+            pltpu.SemaphoreType.DMA((chunks, PIECES)),
+            pltpu.SemaphoreType.DMA((chunks, PIECES)),
+            pltpu.SemaphoreType.DMA((chunks, PIECES)),
+            pltpu.SemaphoreType.DMA((chunks, PIECES)),
             pltpu.SemaphoreType.DMA((micro,)),
             pltpu.SemaphoreType.DMA((micro,)),
             pltpu.SemaphoreType.DMA((micro,)),

time: 179 us -> 158 us (0.88)
  Pallas kernels: 177 us -> 156 us
    pallas_call x1, Pallas kernels: 172 us -> 150 us  [run_chain(): pl.pallas_call(chain_kernel, out_shape=jax.ShapeDtypeStruct(exchange, BF1...]
where the time goes in v2:
time: 158 us
  Pallas kernels  156 us (99%)
    pallas_call x1, Pallas kernels, run_chain(): pl.pallas_call(chain_kernel, out_shape=jax.ShapeDtypeStruct(exchange, BF1...  150 us
    pallas_call x1, Pallas kernels, place(): pl.pallas_call(place_kernel, grid=(steps + 1,), in_specs=[pl.BlockSpec(me...  5.4 us

profile of v2, /device:TPU:1, one launch (start us, length us, event | category | flops | bytes accessed | tf_op | source)
XLA Modules:
  0.0 157.6 jit_solution(17571880996321297794)
XLA Ops:
  0.6 0.0 copy-start.1
  0.6 0.0 copy-start.2
  0.7 150.1 %chain.1 = bf16[2,32,96,128]{3,2,1,0:T(8,128)(2,1)} custom-call(bf16[256,5120]{1,0:T(8,128)(2,1)} %bitcast.22, bf16[256,5120]{1,0:T(8,128)(2,1)} %bitcast.23, f32[1,5120]{1,0:T(1,128)} %gains.1, bf16[5120,512]{1,0:T(8,128)(2,1)} %bitcast.20, bf16[512,5120]{1,0:T(8,128)(2,1)} %bitcast.21, bf16[160,64,128]{2,1,0:T(8,128)(2,1)} %bitcast.24, ...), custom_call_target="tpu_custom_call" | custom-call | tf_op jit(solution)/shard_map/chain/pallas_call | solution.py:422
  150.8 0.0 copy-done.1
  150.8 0.0 copy-done.2
  150.8 0.0 copy-start
  150.8 1.4 copy-done
  152.2 5.4 %place.1 = (f32[2,80,64,128]{3,2,1,0:T(8,128)}, f32[16,64,128]{2,1,0:T(8,128)}) custom-call(s32[2,32]{1,0:T(2,128)S(1)} %copy-done.1, s32[128]{0:T(128)S(1)} %copy-done.2, bf16[64,96,128]{2,1,0:T(8,128)(2,1)S(1)} %bitcast.19), custom_call_target="tpu_custom_call" | custom-call | tf_op jit(solution)/shard_map/place/pallas_call | solution.py:498
Async XLA Ops:
  0.6 150.1 %copy-start.1 = (s32[2,32]{1,0:T(2,128)S(1)}, s32[2,32]{1,0:T(2,128)}, u32[]{:S(2)}) copy-start(s32[2,32]{1,0:T(2,128)} %criterion.3) | copy-start | bytes 772
  0.6 150.1 %copy-start.2 = (s32[128]{0:T(128)S(1)}, s32[128]{0:T(128)}, u32[]{:S(2)}) copy-start(s32[128]{0:T(128)} %slot_of.3) | copy-start | bytes 1540
  150.8 1.4 copy-start

commit v3 on v2

--- a/solution.py
+++ b/solution.py
@@ -6,7 +6,7 @@
 from jax.sharding import PartitionSpec as P
 
 EPSILON = 1e-06
-CHUNK = 32
+CHUNK = 16
 TILE = 512
 GROUP = 16
 PIECES = 2
@@ -113,8 +113,8 @@
             [(down, down_ref), (up, up_ref), (w_value, value_ref), (w_out, out_ref)]
         )
     ]
-    for load in loads:
-        load.start()
+    loads[0].start()
+    loads[1].start()
 
     def tiles_of(piece):
         base = piece * piece_width
@@ -122,6 +122,32 @@
 
     def chunk_rows(c):
         return pl.ds(pl.multiple_of(c * CHUNK, CHUNK), CHUNK)
+
+    barrier = pltpu.get_barrier_semaphore()
+
+    def greet(k, carry):
+        pl.semaphore_signal(
+            barrier,
+            inc=1,
+            device_id={"dp": lax.rem(me + k, peers)},
+            device_id_type=pl.DeviceIdType.MESH,
+        )
+        return carry
+
+    lax.fori_loop(1, peers, greet, 0)
+    for step in (1, sections - 1):
+        pl.semaphore_signal(
+            barrier,
+            inc=1,
+            device_id={"section": lax.rem(section + step, sections)},
+            device_id_type=pl.DeviceIdType.MESH,
+        )
+
+    fill_picks(picks, criterion, slot_of)
+    chosen = picks[...].astype(BF16)
+    loads[0].wait()
+    loads[1].wait()
+    loads[2].start()
 
     @pl.when(first)
     def _():
@@ -145,30 +171,7 @@
                     g_recv_sem.at[c, piece],
                 ).start()
 
-    barrier = pltpu.get_barrier_semaphore()
-
-    def greet(k, carry):
-        pl.semaphore_signal(
-            barrier,
-            inc=1,
-            device_id={"dp": lax.rem(me + k, peers)},
-            device_id_type=pl.DeviceIdType.MESH,
-        )
-        return carry
-
-    lax.fori_loop(1, peers, greet, 0)
-    for step in (1, sections - 1):
-        pl.semaphore_signal(
-            barrier,
-            inc=1,
-            device_id={"section": lax.rem(section + step, sections)},
-            device_id_type=pl.DeviceIdType.MESH,
-        )
-
-    fill_picks(picks, criterion, slot_of)
-    chosen = picks[...].astype(BF16)
-    loads[0].wait()
-    loads[1].wait()
+    loads[3].start()
     for start in range(0, down_half, GROUP):
         pair = jnp.concatenate(
             [down_ref[start : start + GROUP], down_ref[down_half + start : down_half + start + GROUP]],
@@ -211,7 +214,6 @@
         spread(m, panel_send, panel_recv, panel_send_sem, panel_recv_sem)
 
     loads[2].wait()
-    loads[3].wait()
 
     def unpack(m):
         wait_for(panel_recv.at[m], panel_recv_sem.at[m])
@@ -264,7 +266,7 @@
         inverse[here, :] = jnp.broadcast_to(factor, (CHUNK, LANES))
         mixed_ref[here, :] = mixed
 
-        @pl.when(c % per_block == 0)
+        @pl.when(first & (c % per_block == 0))
         def _():
             unpack(m)
 
@@ -285,16 +287,20 @@
                     h_out[here, tile] = (h_in[here, tile].astype(F32) + added).astype(BF16)
                 send_piece(h_out, h_in, c, piece, h_send_sem, h_recv_sem, section + 1)
 
-    def backward(c):
-        m = c // per_block
+    def pull(c, carry):
         here = chunk_rows(c)
         pulled = jnp.zeros((CHUNK, value_width), F32)
         for piece in range(PIECES):
             wait_for(g_in.at[here, pieces[piece]], g_recv_sem.at[c, piece])
             for tile in tiles_of(piece):
                 pulled += dot(g_in[here, tile], out_turned[tile, :])
-        pulled = pulled.astype(BF16)
-        value_grad[here, :] = pulled
+        value_grad[here, :] = pulled.astype(BF16)
+        return carry
+
+    def backward(c):
+        m = c // per_block
+        here = chunk_rows(c)
+        pulled = value_grad[here, :]
         narrow = dot(pulled, panel_up[m])
         narrow = narrow + swap_halves(narrow)
         factor = inverse[here, 0:1]
@@ -355,15 +361,23 @@
 
         lax.fori_loop(0, width // TILE, one, 0)
 
-    lag = jnp.where(first, chunks, jnp.where(last, 0, (sections - 1 - section) * 3))
+    lag = jnp.where(first, chunks, jnp.where(last, 0, (sections - 1 - section) * 4))
     lag = jnp.minimum(lag, chunks)
 
+    loads[3].wait()
     turn_at = jnp.where(first, chunks, 0)
+
+    drawn = jnp.minimum(jnp.maximum(lag + per_block, chunks + 1), chunks + lag) - 1
 
     def step(t, carry):
         @pl.when(t == turn_at)
         def _():
             turn()
+            lax.fori_loop(0, jnp.where(last, chunks, 0), pull, 0)
+
+        @pl.when((section > 0) & (t < micro))
+        def _():
+            unpack(t)
 
         @pl.when(t < chunks)
         def _():
@@ -373,11 +387,16 @@
 
         @pl.when((c >= 0) & (c < chunks))
         def _():
+            lax.fori_loop(c, jnp.where(last, c, c + 1), pull, 0)
             backward(c)
 
-            @pl.when(c % per_block == per_block - 1)
-            def _():
-                products(c // per_block)
+        @pl.when(t == drawn)
+        def _():
+            products(0)
+
+        @pl.when(t == chunks + lag - 1)
+        def _():
+            products(1)
 
         return carry
 
@@ -467,17 +486,24 @@
     )(tokens, cotangent, gains, w_value, w_out, down, up, criterion, slot_of)
 
 
-def place_kernel(criterion, slot_of, parts, down, up, picks):
+def place_kernel(criterion, slot_of, parts, down, up, picks, held, sems):
     step = pl.program_id(0)
     pairs = parts.shape[0]
     up_half = up.shape[0] // 2
 
+    def load(index):
+        rows = pl.ds(pl.multiple_of(index * GROUP, GROUP), GROUP)
+        return pltpu.make_async_copy(parts.at[:, rows], held.at[index], sems.at[index])
+
     @pl.when(step == 0)
     def _():
+        for index in range(held.shape[0]):
+            load(index).start()
         fill_picks(picks, criterion, slot_of)
 
+    load(step).wait()
     chosen = picks[...].astype(BF16)
-    flat = parts[...].reshape(pairs, GROUP * LANES)
+    flat = held[step].reshape(pairs, GROUP * LANES)
     summed = dot_tn(flat, chosen).reshape(GROUP, 2, LANES // 2, picks.shape[1])
 
     @pl.when(step < pl.num_programs(0) - 1)
@@ -501,7 +527,7 @@
         in_specs=[
             pl.BlockSpec(memory_space=pltpu.SMEM),
             pl.BlockSpec(memory_space=pltpu.SMEM),
-            pl.BlockSpec((pairs, GROUP, LANES), lambda i: (0, i, 0)),
+            pl.BlockSpec(memory_space=pltpu.HBM),
         ],
         out_specs=[
             pl.BlockSpec((2, GROUP, rank, slots), lambda i: (0, jnp.minimum(i, steps - 1), 0, 0)),
@@ -511,8 +537,12 @@
             jax.ShapeDtypeStruct((2, down_half, rank, slots), F32),
             jax.ShapeDtypeStruct((value_rows, rank, slots), F32),
         ],
-        scratch_shapes=[pltpu.VMEM((pairs, slots), F32)],
-        compiler_params=pltpu.CompilerParams(vmem_limit_bytes=32 * 1024 * 1024),
+        scratch_shapes=[
+            pltpu.VMEM((pairs, slots), F32),
+            pltpu.VMEM((steps + 1, pairs, GROUP, LANES), BF16),
+            pltpu.SemaphoreType.DMA((steps + 1,)),
+        ],
+        compiler_params=pltpu.CompilerParams(vmem_limit_bytes=60 * 1024 * 1024),
         name="place",
     )(criterion, slot_of, parts)
     return down.reshape(feature_rows, rank, slots), up

time: 158 us -> 149 us (0.943)
  Pallas kernels: 156 us -> 148 us
    pallas_call x1, Pallas kernels: 150 us -> 141 us  [run_chain(): pl.pallas_call(chain_kernel, out_shape=jax.ShapeDtypeStruct(exchange, BF1...]
where the time goes in v3:
time: 149 us; the launch traced here: 148 us
  Pallas kernels  148 us (99%)
    pallas_call x1, Pallas kernels, run_chain(): pl.pallas_call(chain_kernel, out_shape=jax.ShapeDtypeStruct(exchange, BF1...  141 us
    pallas_call x1, Pallas kernels, place(): pl.pallas_call(place_kernel, grid=(steps + 1,), in_specs=[pl.BlockSpec(me...  6.53 us

profile of v3, /device:TPU:1, one launch (start us, length us, event | category | flops | bytes accessed | tf_op | source)
XLA Modules:
  0.0 148.4 jit_solution(15604867073042835140)
XLA Ops:
  0.6 141.2 %chain.1 = bf16[2,32,96,128]{3,2,1,0:T(8,128)(2,1)} custom-call(bf16[256,5120]{1,0:T(8,128)(2,1)} %bitcast.22, bf16[256,5120]{1,0:T(8,128)(2,1)} %bitcast.23, f32[1,5120]{1,0:T(1,128)} %gains.1, bf16[5120,512]{1,0:T(8,128)(2,1)} %bitcast.20, bf16[512,5120]{1,0:T(8,128)(2,1)} %bitcast.21, bf16[160,64,128]{2,1,0:T(8,128)(2,1)} %bitcast.24, ...), custom_call_target="tpu_custom_call" | custom-call | tf_op jit(solution)/shard_map/chain/pallas_call | solution.py:441
  141.9 6.5 %place.1 = (f32[2,80,64,128]{3,2,1,0:T(8,128)}, f32[16,64,128]{2,1,0:T(8,128)}) custom-call(s32[2,32]{1,0:T(2,128)} %criterion.3, s32[128]{0:T(128)} %slot_of.3, bf16[64,96,128]{2,1,0:T(8,128)(2,1)} %bitcast.19), custom_call_target="tpu_custom_call" | custom-call | tf_op jit(solution)/shard_map/place/pallas_call | solution.py:524

commit v4 on v3

--- a/solution.py
+++ b/solution.py
@@ -51,13 +51,13 @@
     criterion,
     slot_of,
     grad_recv,
+    picks,
     value_ref,
     out_ref,
     value_turned,
     out_turned,
     down_ref,
     up_ref,
-    picks,
     h_in,
     h_out,
     g_in,
@@ -73,7 +73,7 @@
     panel_recv,
     panel_down,
     panel_up,
-    product_down,
+    lifted,
     product_up,
     grad_send,
     load_sem,
@@ -191,48 +191,60 @@
 
     pl.semaphore_wait(barrier, peers + 1)
 
+    def hand(m, peer, source, target, send_sem, recv_sem):
+        pltpu.make_async_remote_copy(
+            src_ref=source.at[m, peer],
+            dst_ref=target.at[m, me],
+            send_sem=send_sem.at[m],
+            recv_sem=recv_sem.at[m],
+            device_id={"dp": peer},
+            device_id_type=pl.DeviceIdType.MESH,
+        ).start()
+
+    def keep(m, source, target, recv_sem):
+        pltpu.make_async_copy(source.at[m, me], target.at[m, me], recv_sem.at[m]).start()
+
     def spread(m, source, target, send_sem, recv_sem):
         def send(k, carry):
-            peer = lax.rem(me + k, peers)
-            pltpu.make_async_remote_copy(
-                src_ref=source.at[m, peer],
-                dst_ref=target.at[m, me],
-                send_sem=send_sem.at[m],
-                recv_sem=recv_sem.at[m],
-                device_id={"dp": peer},
-                device_id_type=pl.DeviceIdType.MESH,
-            ).start()
+            hand(m, lax.rem(me + k, peers), source, target, send_sem, recv_sem)
             return carry
 
-        pltpu.make_async_copy(source.at[m, me], target.at[m, me], recv_sem.at[m]).start()
+        keep(m, source, target, recv_sem)
         lax.fori_loop(1, peers, send, 0)
 
     def wait_for(ref, sem):
         pltpu.make_async_copy(ref, ref, sem).wait()
 
-    for m in range(micro):
-        spread(m, panel_send, panel_recv, panel_send_sem, panel_recv_sem)
+    spread(0, panel_send, panel_recv, panel_send_sem, panel_recv_sem)
 
     loads[2].wait()
+
+    near = lax.broadcasted_iota(jnp.int32, (down_half, LANES), 1) < LANES // 2
+    near_up = near[0:up_half]
+    near_row = near[0:CHUNK]
 
     def unpack(m):
         wait_for(panel_recv.at[m], panel_recv_sem.at[m])
-        near = lax.broadcasted_iota(jnp.int32, (down_half, LANES), 1) < LANES // 2
-        near_up = lax.broadcasted_iota(jnp.int32, (up_half, LANES), 1) < LANES // 2
+
+        @pl.when(m < micro - 1)
+        def _():
+            spread(m + 1, panel_send, panel_recv, panel_send_sem, panel_recv_sem)
 
         def one(source, carry):
             at = pl.multiple_of(source * feature_rows, 2 * GROUP)
             part = panel_recv[m, source, 0:down_half, :]
-            none = jnp.zeros_like(part)
-            panel_down[m, pl.ds(at, down_half), :] = jnp.where(near, part, none)
-            panel_down[m, pl.ds(at + down_half, down_half), :] = jnp.where(near, none, part)
-            at = pl.multiple_of(source * value_rows, GROUP)
-            part = panel_recv[m, source, down_half:packed, :].astype(F32)[0:up_half]
-            both = [jnp.where(near_up, part, 0.0), jnp.where(near_up, 0.0, part)]
-            panel_up[m, pl.ds(at, value_rows), :] = jnp.concatenate(both, axis=0).astype(BF16)
+            other = panel_recv[m, source + peers // 2, 0:down_half, :]
+            crossed = swap_halves(jnp.where(near, other, part))
+            panel_down[m, pl.ds(at, down_half), :] = jnp.where(near, part, crossed)
+            panel_down[m, pl.ds(at + down_half, down_half), :] = jnp.where(near, crossed, other)
+            for place in (source, source + peers // 2):
+                at = pl.multiple_of(place * value_rows, GROUP)
+                part = panel_recv[m, place, down_half:packed, :].astype(F32)[0:up_half]
+                both = [jnp.where(near_up, part, 0.0), jnp.where(near_up, 0.0, part)]
+                panel_up[m, pl.ds(at, value_rows), :] = jnp.concatenate(both, axis=0).astype(BF16)
             return carry
 
-        lax.fori_loop(0, peers, one, 0)
+        lax.fori_loop(0, peers // 2, one, 0)
 
     def send_piece(source, target, c, piece, send_sem, recv_sem, to):
         here = chunk_rows(c)
@@ -270,10 +282,11 @@
         def _():
             unpack(m)
 
-        narrow = jnp.zeros((CHUNK, LANES), F32)
-        for piece in range(PIECES):
-            for tile in tiles_of(piece):
-                narrow += dot(scaled[here, tile], panel_down[m, tile, :])
+        narrow = jnp.zeros((2 * CHUNK, LANES), F32)
+        for tile, far in zip(tiles_of(0), tiles_of(1)):
+            both = jnp.concatenate([scaled[here, tile], scaled[here, far]], axis=0)
+            narrow += dot(both, panel_down[m, tile, :])
+        narrow = jnp.where(near_row, narrow[0:CHUNK], narrow[CHUNK : 2 * CHUNK])
         narrow_ref[here, :] = narrow
         narrow = ((narrow + swap_halves(narrow)) * factor).astype(BF16)
         low[here, :] = narrow
@@ -314,10 +327,15 @@
             along = held.astype(F32) * narrow_ref[here, :]
             moment += jnp.sum(along, axis=1, keepdims=True)
             bend = factor * factor * factor * (moment / width)
+            none = jnp.zeros_like(held)
+            both = [jnp.where(near_row, held, none), jnp.where(near_row, none, held)]
+            both = jnp.concatenate(both, axis=0)
+            for tile in tiles_of(0):
+                lifted[:, tile] = dot_nt(both, panel_down[m, tile, :])
             for piece in range(PIECES):
-                for tile in tiles_of(piece):
+                for near_tile, tile in zip(tiles_of(0), tiles_of(piece)):
                     part = dot(pulled, value_turned[:, tile])
-                    part += dot_nt(held, panel_down[m, tile, :])
+                    part += lifted[piece * CHUNK : (piece + 1) * CHUNK, near_tile]
                     result = (
                         g_in[here, tile].astype(F32)
                         + factor * (part * gains[:, tile])
@@ -328,29 +346,39 @@
 
     def products(m):
         here = pl.ds(pl.multiple_of(m * block, block), block)
-        for start in range(0, width, TILE):
-            tile = slice(start, start + TILE)
-            product_down[tile, :] = dot_tn(scaled[here, tile], low_grad[here, :]).astype(BF16)
         product_up[...] = dot_tn(value_grad[here, :], low[here, :])
-        near = lax.broadcasted_iota(jnp.int32, (down_half, LANES), 1) < LANES // 2
-        near_up = lax.broadcasted_iota(jnp.int32, (up_half, LANES), 1) < LANES // 2
-
-        def pack(peer, carry):
-            at = pl.multiple_of(peer * feature_rows, 2 * GROUP)
-            part = product_down[pl.ds(at, down_half), :]
-            other = product_down[pl.ds(at + down_half, down_half), :]
-            grad_send[m, peer, 0:down_half, :] = jnp.where(near, part, other)
-            at = pl.multiple_of(peer * value_rows, GROUP)
-            part = product_up[pl.ds(at, value_rows), :]
-            part = jnp.where(near_up, part[0:up_half], part[up_half:value_rows])
-            if packed - down_half > up_half:
-                rest = jnp.zeros((packed - down_half - up_half, LANES), F32)
-                part = jnp.concatenate([part, rest], axis=0)
-            grad_send[m, peer, down_half:packed, :] = part.astype(BF16)
+        several = min(4, peers)
+        span = several * feature_rows
+
+        def group(k, carry):
+            which = lax.rem(me // several + k, peers // several)
+            columns = pl.ds(pl.multiple_of(which * span, LANES), span)
+            product = dot_tn(scaled[here, columns], low_grad[here, :]).astype(BF16)
+            for q in range(several):
+                peer = which * several + q
+                at = q * feature_rows
+                part = product[at : at + down_half]
+                other = product[at + down_half : at + feature_rows]
+                grad_send[m, peer, 0:down_half, :] = jnp.where(near, part, other)
+                at = pl.multiple_of(peer * value_rows, GROUP)
+                part = product_up[pl.ds(at, value_rows), :]
+                part = jnp.where(near_up, part[0:up_half], part[up_half:value_rows])
+                if packed - down_half > up_half:
+                    rest = jnp.zeros((packed - down_half - up_half, LANES), F32)
+                    part = jnp.concatenate([part, rest], axis=0)
+                grad_send[m, peer, down_half:packed, :] = part.astype(BF16)
+
+                @pl.when(peer != me)
+                def _():
+                    hand(m, peer, grad_send, grad_recv, grad_send_sem, grad_recv_sem)
+
+                @pl.when(peer == me)
+                def _():
+                    keep(m, grad_send, grad_recv, grad_recv_sem)
+
             return carry
 
-        lax.fori_loop(0, peers, pack, 0)
-        spread(m, grad_send, grad_recv, grad_send_sem, grad_recv_sem)
+        lax.fori_loop(0, peers // several, group, 0)
 
     def turn():
         def one(index, carry):
@@ -375,9 +403,9 @@
             turn()
             lax.fori_loop(0, jnp.where(last, chunks, 0), pull, 0)
 
-        @pl.when((section > 0) & (t < micro))
-        def _():
-            unpack(t)
+        @pl.when((section > 0) & ((t == 0) | (t == per_block // 2)))
+        def _():
+            unpack(jnp.where(t == 0, 0, 1))
 
         @pl.when(t < chunks)
         def _():
@@ -440,9 +468,15 @@
     exchange = (micro, peers, packed, LANES)
     return pl.pallas_call(
         chain_kernel,
-        out_shape=jax.ShapeDtypeStruct(exchange, BF16),
+        out_shape=[
+            jax.ShapeDtypeStruct(exchange, BF16),
+            jax.ShapeDtypeStruct((micro * criterion.shape[1], slots), F32),
+        ],
         in_specs=spaces,
-        out_specs=pl.BlockSpec(memory_space=pl.ANY),
+        out_specs=[
+            pl.BlockSpec(memory_space=pl.ANY),
+            pl.BlockSpec(memory_space=pltpu.VMEM),
+        ],
         scratch_shapes=[
             pltpu.VMEM(w_value.shape, BF16),
             pltpu.VMEM(w_out.shape, BF16),
@@ -450,7 +484,6 @@
             pltpu.VMEM(w_value.shape, BF16),
             pltpu.VMEM(down.shape, BF16),
             pltpu.VMEM(up.shape, BF16),
-            pltpu.VMEM((micro * criterion.shape[1], slots), F32),
             row_buffer,
             row_buffer,
             row_buffer,
@@ -464,9 +497,9 @@
             pltpu.VMEM((rows, LANES), BF16),
             pltpu.VMEM(exchange, BF16),
             pltpu.VMEM(exchange, BF16),
-            pltpu.VMEM((micro, width, LANES), BF16),
+            pltpu.VMEM((micro, width // 2, LANES), BF16),
             pltpu.VMEM((micro, value_width, LANES), BF16),
-            pltpu.VMEM((width, LANES), BF16),
+            pltpu.VMEM((2 * CHUNK, width // 2), F32),
             pltpu.VMEM((value_width, LANES), F32),
             pltpu.VMEM(exchange, BF16),
             pltpu.SemaphoreType.DMA((4,)),
@@ -486,66 +519,71 @@
     )(tokens, cotangent, gains, w_value, w_out, down, up, criterion, slot_of)
 
 
-def place_kernel(criterion, slot_of, parts, down, up, picks, held, sems):
-    step = pl.program_id(0)
+def place_kernel(picks, parts, down, up, chosen, held, down_out, up_out, pick_sem, load_sem, store_sem):
     pairs = parts.shape[0]
+    groups = held.shape[0]
     up_half = up.shape[0] // 2
-
-    def load(index):
-        rows = pl.ds(pl.multiple_of(index * GROUP, GROUP), GROUP)
-        return pltpu.make_async_copy(parts.at[:, rows], held.at[index], sems.at[index])
-
-    @pl.when(step == 0)
-    def _():
-        for index in range(held.shape[0]):
-            load(index).start()
-        fill_picks(picks, criterion, slot_of)
-
-    load(step).wait()
-    chosen = picks[...].astype(BF16)
-    flat = held[step].reshape(pairs, GROUP * LANES)
-    summed = dot_tn(flat, chosen).reshape(GROUP, 2, LANES // 2, picks.shape[1])
-
-    @pl.when(step < pl.num_programs(0) - 1)
-    def _():
-        down[0] = summed[:, 0]
-        down[1] = summed[:, 1]
-
-    @pl.when(step == pl.num_programs(0) - 1)
-    def _():
-        up[0:up_half] = summed[0:up_half, 0]
-        up[up_half : 2 * up_half] = summed[0:up_half, 1]
-
-
-def place(criterion, slot_of, parts, feature_rows, value_rows, slots, rank):
-    pairs = parts.shape[0]
-    down_half = feature_rows // 2
-    steps = down_half // GROUP
-    down, up = pl.pallas_call(
+    half = down.shape[0] // 2
+    pick_load = pltpu.make_async_copy(picks, chosen, pick_sem)
+    pick_load.start()
+    loads = [
+        pltpu.make_async_copy(
+            parts.at[:, pl.ds(index * GROUP, GROUP)], held.at[index], load_sem.at[index]
+        )
+        for index in range(groups)
+    ]
+    for load in loads:
+        load.start()
+    pick_load.wait()
+    stores = []
+    for index in range(groups):
+        loads[index].wait()
+        flat = held[index].reshape(pairs, GROUP * LANES)
+        summed = dot_tn(flat, chosen[...].astype(BF16))
+        summed = summed.reshape(GROUP, 2, LANES // 2, chosen.shape[1])
+        for side in range(2):
+            if index < groups - 1:
+                at = pl.ds(side * half + index * GROUP, GROUP)
+                down_out[at] = summed[:, side]
+                store = pltpu.make_async_copy(
+                    down_out.at[at], down.at[at], store_sem.at[index, side]
+                )
+            else:
+                at = pl.ds(side * up_half, up_half)
+                up_out[at] = summed[0:up_half, side]
+                store = pltpu.make_async_copy(up_out.at[at], up.at[at], store_sem.at[index, side])
+            store.start()
+            stores.append(store)
+    for store in stores:
+        store.wait()
+
+
+def place(picks, parts, feature_rows, value_rows, rank):
+    pairs, packed = parts.shape[0:2]
+    slots = picks.shape[1]
+    groups = packed // GROUP
+    down_shape = (feature_rows, rank, slots)
+    up_shape = (value_rows, rank, slots)
+    return pl.pallas_call(
         place_kernel,
-        grid=(steps + 1,),
-        in_specs=[
-            pl.BlockSpec(memory_space=pltpu.SMEM),
-            pl.BlockSpec(memory_space=pltpu.SMEM),
-            pl.BlockSpec(memory_space=pltpu.HBM),
-        ],
-        out_specs=[
-            pl.BlockSpec((2, GROUP, rank, slots), lambda i: (0, jnp.minimum(i, steps - 1), 0, 0)),
-            pl.BlockSpec((value_rows, rank, slots), lambda i: (0, 0, 0)),
-        ],
+        in_specs=[pl.BlockSpec(memory_space=pltpu.HBM)] * 2,
+        out_specs=[pl.BlockSpec(memory_space=pl.ANY)] * 2,
         out_shape=[
-            jax.ShapeDtypeStruct((2, down_half, rank, slots), F32),
-            jax.ShapeDtypeStruct((value_rows, rank, slots), F32),
+            jax.ShapeDtypeStruct(down_shape, F32),
+            jax.ShapeDtypeStruct(up_shape, F32),
         ],
         scratch_shapes=[
             pltpu.VMEM((pairs, slots), F32),
-            pltpu.VMEM((steps + 1, pairs, GROUP, LANES), BF16),
-            pltpu.SemaphoreType.DMA((steps + 1,)),
+            pltpu.VMEM((groups, pairs, GROUP, LANES), BF16),
+            pltpu.VMEM(down_shape, F32),
+            pltpu.VMEM(up_shape, F32),
+            pltpu.SemaphoreType.DMA,
+            pltpu.SemaphoreType.DMA((groups,)),
+            pltpu.SemaphoreType.DMA((groups, 2)),
         ],
         compiler_params=pltpu.CompilerParams(vmem_limit_bytes=60 * 1024 * 1024),
         name="place",
-    )(criterion, slot_of, parts)
-    return down.reshape(feature_rows, rank, slots), up
+    )(picks, parts)
 
 
 def on_device(
@@ -562,7 +600,7 @@
     micro, block, width = tokens.shape
     down = jnp.transpose(adapter_down[0], (1, 2, 0))
     up = jnp.transpose(adapter_up[0], (1, 2, 0))
-    parts = run_chain(
+    parts, picks = run_chain(
         tokens.reshape(micro * block, width),
         cotangent.reshape(micro * block, width),
         norm_gain,
@@ -574,9 +612,7 @@
         slot_of,
     )
     parts = parts.reshape((parts.shape[0] * parts.shape[1],) + parts.shape[2:])
-    grad_down, grad_up = place(
-        criterion, slot_of, parts, down.shape[0], up.shape[0], down.shape[2], down.shape[1]
-    )
+    grad_down, grad_up = place(picks, parts, down.shape[0], up.shape[0], down.shape[1])
     return (jnp.transpose(grad_down, (2, 0, 1))[None], jnp.transpose(grad_up, (2, 0, 1))[None])
 
 

time: 149 us -> 143 us (0.960)
  Pallas kernels: 148 us -> 142 us
    pallas_call x2, Pallas kernels: 148 us -> 142 us  [the longest x1 137 us: run_chain(): pl.pallas_call(chain_kernel, out_shape=[jax.ShapeDtypeStruct(exchange, BF...]
where the time goes in v4:
time: 143 us
  Pallas kernels  142 us (99%)
    pallas_call x1, Pallas kernels, run_chain(): pl.pallas_call(chain_kernel, out_shape=[jax.ShapeDtypeStruct(exchange, BF...  137 us
    pallas_call x1, Pallas kernels, place(): pl.pallas_call(place_kernel, in_specs=[pl.BlockSpec(memory_space=pltpu.HB...  4.89 us

profile of v4, /device:TPU:1, one launch (start us, length us, event | category | flops | bytes accessed | tf_op | source)
XLA Modules:
  0.0 142.7 jit_solution(13379988729874814231)
XLA Ops:
  0.6 137.2 %chain.1 = (bf16[2,32,96,128]{3,2,1,0:T(8,128)(2,1)}, f32[64,128]{1,0:T(8,128)}) custom-call(bf16[256,5120]{1,0:T(8,128)(2,1)} %bitcast.19, bf16[256,5120]{1,0:T(8,128)(2,1)} %bitcast.20, f32[1,5120]{1,0:T(1,128)} %gains.1, bf16[5120,512]{1,0:T(8,128)(2,1)} %bitcast.17, bf16[512,5120]{1,0:T(8,128)(2,1)} %bitcast.18, bf16[160,64,128]{2,1,0:T(8,128)(2,1)} %bitcast.21, ...), custom_call_target="tpu_custom_call" | custom-call | tf_op jit(solution)/shard_map/chain/pallas_call | solution.py:469
  137.8 4.9 %place.1 = (f32[160,64,128]{2,1,0:T(8,128)}, f32[16,64,128]{2,1,0:T(8,128)}) custom-call(f32[64,128]{1,0:T(8,128)} %get-tuple-element.6.picks, bf16[64,96,128]{2,1,0:T(8,128)(2,1)} %bitcast.22), custom_call_target="tpu_custom_call" | custom-call | tf_op jit(solution)/shard_map/place/pallas_call | solution.py:567

commit v5 on v4

--- a/solution.py
+++ b/solution.py
@@ -73,7 +73,6 @@
     panel_recv,
     panel_down,
     panel_up,
-    lifted,
     product_up,
     grad_send,
     load_sem,
@@ -191,31 +190,34 @@
 
     pl.semaphore_wait(barrier, peers + 1)
 
-    def hand(m, peer, source, target, send_sem, recv_sem):
+    def hand(m, peer, source, target, send_sem, landed):
         pltpu.make_async_remote_copy(
             src_ref=source.at[m, peer],
             dst_ref=target.at[m, me],
             send_sem=send_sem.at[m],
-            recv_sem=recv_sem.at[m],
+            recv_sem=landed,
             device_id={"dp": peer},
             device_id_type=pl.DeviceIdType.MESH,
         ).start()
 
-    def keep(m, source, target, recv_sem):
-        pltpu.make_async_copy(source.at[m, me], target.at[m, me], recv_sem.at[m]).start()
-
-    def spread(m, source, target, send_sem, recv_sem):
+    def keep(m, source, target, landed):
+        pltpu.make_async_copy(source.at[m, me], target.at[m, me], landed).start()
+
+    def spread_panels(m):
+        landed = panel_recv_sem.at[m, me]
+
         def send(k, carry):
-            hand(m, lax.rem(me + k, peers), source, target, send_sem, recv_sem)
+            peer = lax.rem(me + k // 2 + k % 2 * (peers // 2), peers)
+            hand(m, peer, panel_send, panel_recv, panel_send_sem, landed)
             return carry
 
-        keep(m, source, target, recv_sem)
+        keep(m, panel_send, panel_recv, landed)
         lax.fori_loop(1, peers, send, 0)
 
     def wait_for(ref, sem):
         pltpu.make_async_copy(ref, ref, sem).wait()
 
-    spread(0, panel_send, panel_recv, panel_send_sem, panel_recv_sem)
+    spread_panels(0)
 
     loads[2].wait()
 
@@ -224,13 +226,10 @@
     near_row = near[0:CHUNK]
 
     def unpack(m):
-        wait_for(panel_recv.at[m], panel_recv_sem.at[m])
-
-        @pl.when(m < micro - 1)
-        def _():
-            spread(m + 1, panel_send, panel_recv, panel_send_sem, panel_recv_sem)
-
-        def one(source, carry):
+        def one(k, carry):
+            source = lax.rem(me - k + peers, peers // 2)
+            for place in (source, source + peers // 2):
+                wait_for(panel_recv.at[m, place], panel_recv_sem.at[m, place])
             at = pl.multiple_of(source * feature_rows, 2 * GROUP)
             part = panel_recv[m, source, 0:down_half, :]
             other = panel_recv[m, source + peers // 2, 0:down_half, :]
@@ -246,6 +245,10 @@
 
         lax.fori_loop(0, peers // 2, one, 0)
 
+        @pl.when(m < micro - 1)
+        def _():
+            spread_panels(m + 1)
+
     def send_piece(source, target, c, piece, send_sem, recv_sem, to):
         here = chunk_rows(c)
         columns = pieces[piece]
@@ -261,8 +264,14 @@
     def forward(c):
         m = c // per_block
         here = chunk_rows(c)
+
+        @pl.when(first & (c % per_block == 0))
+        def _():
+            unpack(m)
+
         squares = jnp.zeros((CHUNK, LANES), F32)
         mixed = jnp.zeros((CHUNK, value_width), F32)
+        narrow = jnp.zeros((2 * CHUNK, LANES), F32)
         for piece in range(PIECES):
             wait_for(h_in.at[here, pieces[piece]], h_recv_sem.at[c, piece])
             for tile in tiles_of(piece):
@@ -270,30 +279,25 @@
                 square = hidden * hidden
                 for start in range(0, TILE, LANES):
                     squares += square[:, start : start + LANES]
-                part = (hidden * gains[:, tile]).astype(BF16)
-                scaled[here, tile] = part
-                mixed += dot(part, value_ref[tile, :])
+                scaled[here, tile] = (hidden * gains[:, tile]).astype(BF16)
+            if piece == PIECES - 1:
+                for tile, far in zip(tiles_of(0), tiles_of(1)):
+                    both = jnp.concatenate([scaled[here, tile], scaled[here, far]], axis=0)
+                    narrow += dot(both, panel_down[m, tile, :])
+            for tile in tiles_of(piece):
+                mixed += dot(scaled[here, tile], value_ref[tile, :])
         total = jnp.sum(squares, axis=1, keepdims=True)
         factor = lax.rsqrt(total / width + EPSILON)
         inverse[here, :] = jnp.broadcast_to(factor, (CHUNK, LANES))
         mixed_ref[here, :] = mixed
-
-        @pl.when(first & (c % per_block == 0))
-        def _():
-            unpack(m)
-
-        narrow = jnp.zeros((2 * CHUNK, LANES), F32)
-        for tile, far in zip(tiles_of(0), tiles_of(1)):
-            both = jnp.concatenate([scaled[here, tile], scaled[here, far]], axis=0)
-            narrow += dot(both, panel_down[m, tile, :])
         narrow = jnp.where(near_row, narrow[0:CHUNK], narrow[CHUNK : 2 * CHUNK])
         narrow_ref[here, :] = narrow
         narrow = ((narrow + swap_halves(narrow)) * factor).astype(BF16)
         low[here, :] = narrow
+        values = (mixed * factor + dot_nt(narrow, panel_up[m])).astype(BF16)
 
         @pl.when(section < sections - 1)
         def _():
-            values = (mixed * factor + dot_nt(narrow, panel_up[m])).astype(BF16)
             for piece in range(PIECES):
                 for tile in tiles_of(piece):
                     added = dot(values, out_ref[:, tile])
@@ -310,18 +314,27 @@
         value_grad[here, :] = pulled.astype(BF16)
         return carry
 
+    def lower(c, pulled):
+        here = chunk_rows(c)
+        narrow = dot(pulled, panel_up[c // per_block])
+        narrow = narrow + swap_halves(narrow)
+        factor = inverse[here, 0:1]
+        low_grad[here, :] = (narrow * factor).astype(BF16)
+        return narrow.astype(BF16), factor
+
     def backward(c):
         m = c // per_block
         here = chunk_rows(c)
-        pulled = value_grad[here, :]
-        narrow = dot(pulled, panel_up[m])
-        narrow = narrow + swap_halves(narrow)
-        factor = inverse[here, 0:1]
-        low_grad[here, :] = (narrow * factor).astype(BF16)
+
+        @pl.when(first)
+        def _():
+            lower(c, value_grad[here, :])
 
         @pl.when(section > 0)
         def _():
-            held = narrow.astype(BF16)
+            pulled = value_grad[here, :]
+            held, factor = lower(c, pulled)
+            parts = [dot(pulled, value_turned[:, tile]) for tile in tiles_of(0)]
             along = pulled.astype(F32) * mixed_ref[here, :]
             moment = jnp.sum(along, axis=1, keepdims=True)
             along = held.astype(F32) * narrow_ref[here, :]
@@ -330,12 +343,12 @@
             none = jnp.zeros_like(held)
             both = [jnp.where(near_row, held, none), jnp.where(near_row, none, held)]
             both = jnp.concatenate(both, axis=0)
-            for tile in tiles_of(0):
-                lifted[:, tile] = dot_nt(both, panel_down[m, tile, :])
+            lifts = [dot_nt(both, panel_down[m, tile, :]) for tile in tiles_of(0)]
             for piece in range(PIECES):
-                for near_tile, tile in zip(tiles_of(0), tiles_of(piece)):
-                    part = dot(pulled, value_turned[:, tile])
-                    part += lifted[piece * CHUNK : (piece + 1) * CHUNK, near_tile]
+                if piece > 0:
+                    parts = [dot(pulled, value_turned[:, tile]) for tile in tiles_of(piece)]
+                for part, lift, tile in zip(parts, lifts, tiles_of(piece)):
+                    part += lift[piece * CHUNK : (piece + 1) * CHUNK]
                     result = (
                         g_in[here, tile].astype(F32)
                         + factor * (part * gains[:, tile])
@@ -370,11 +383,11 @@
 
                 @pl.when(peer != me)
                 def _():
-                    hand(m, peer, grad_send, grad_recv, grad_send_sem, grad_recv_sem)
+                    hand(m, peer, grad_send, grad_recv, grad_send_sem, grad_recv_sem.at[m])
 
                 @pl.when(peer == me)
                 def _():
-                    keep(m, grad_send, grad_recv, grad_recv_sem)
+                    keep(m, grad_send, grad_recv, grad_recv_sem.at[m])
 
             return carry
 
@@ -389,7 +402,7 @@
 
         lax.fori_loop(0, width // TILE, one, 0)
 
-    lag = jnp.where(first, chunks, jnp.where(last, 0, (sections - 1 - section) * 4))
+    lag = jnp.where(first, chunks, jnp.where(last, 0, (sections - 1 - section) * 3 + (2 - section)))
     lag = jnp.minimum(lag, chunks)
 
     loads[3].wait()
@@ -415,7 +428,10 @@
 
         @pl.when((c >= 0) & (c < chunks))
         def _():
-            lax.fori_loop(c, jnp.where(last, c, c + 1), pull, 0)
+            @pl.when(section < sections - 1)
+            def _():
+                pull(c, 0)
+
             backward(c)
 
         @pl.when(t == drawn)
@@ -499,7 +515,6 @@
             pltpu.VMEM(exchange, BF16),
             pltpu.VMEM((micro, width // 2, LANES), BF16),
             pltpu.VMEM((micro, value_width, LANES), BF16),
-            pltpu.VMEM((2 * CHUNK, width // 2), F32),
             pltpu.VMEM((value_width, LANES), F32),
             pltpu.VMEM(exchange, BF16),
             pltpu.SemaphoreType.DMA((4,)),
@@ -508,7 +523,7 @@
             pltpu.SemaphoreType.DMA((chunks, PIECES)),
             pltpu.SemaphoreType.DMA((chunks, PIECES)),
             pltpu.SemaphoreType.DMA((micro,)),
-            pltpu.SemaphoreType.DMA((micro,)),
+            pltpu.SemaphoreType.DMA((micro, peers)),
             pltpu.SemaphoreType.DMA((micro,)),
             pltpu.SemaphoreType.DMA((micro,)),
         ],
@@ -535,25 +550,36 @@
     for load in loads:
         load.start()
     pick_load.wait()
+    one = chosen[...].astype(BF16)
+    none = jnp.zeros_like(one)
+    pair_of = jnp.concatenate(
+        [jnp.concatenate([one, none], axis=1), jnp.concatenate([none, one], axis=1)], axis=0
+    )
+    slots = chosen.shape[1]
     stores = []
-    for index in range(groups):
-        loads[index].wait()
-        flat = held[index].reshape(pairs, GROUP * LANES)
-        summed = dot_tn(flat, chosen[...].astype(BF16))
-        summed = summed.reshape(GROUP, 2, LANES // 2, chosen.shape[1])
-        for side in range(2):
-            if index < groups - 1:
-                at = pl.ds(side * half + index * GROUP, GROUP)
-                down_out[at] = summed[:, side]
+    for index in range(0, groups, 2):
+        span = min(2, groups - index)
+        for load in loads[index : index + span]:
+            load.wait()
+        flat = jnp.concatenate([held[index + k] for k in range(span)], axis=0)
+        flat = flat.reshape(span * pairs, GROUP * LANES)
+        summed = dot_tn(flat, pair_of if span == 2 else one)
+        for k in range(span):
+            mine = summed[:, k * slots : (k + 1) * slots].reshape(GROUP, 2, LANES // 2, slots)
+            for side in range(2):
+                if index + k < groups - 1:
+                    at = pl.ds(side * half + (index + k) * GROUP, GROUP)
+                    source, target = down_out, down
+                    down_out[at] = mine[:, side]
+                else:
+                    at = pl.ds(side * up_half, up_half)
+                    source, target = up_out, up
+                    up_out[at] = mine[0:up_half, side]
                 store = pltpu.make_async_copy(
-                    down_out.at[at], down.at[at], store_sem.at[index, side]
+                    source.at[at], target.at[at], store_sem.at[index + k, side]
                 )
-            else:
-                at = pl.ds(side * up_half, up_half)
-                up_out[at] = summed[0:up_half, side]
-                store = pltpu.make_async_copy(up_out.at[at], up.at[at], store_sem.at[index, side])
-            store.start()
-            stores.append(store)
+                store.start()
+                stores.append(store)
     for store in stores:
         store.wait()
 

time: 143 us -> 138 us (0.965)
  Pallas kernels: 142 us -> 137 us
    pallas_call x1, Pallas kernels: 137 us -> 133 us  [run_chain(): pl.pallas_call(chain_kernel, out_shape=[jax.ShapeDtypeStruct(exchange, BF...]
where the time goes in v5:
time: 138 us
  Pallas kernels  137 us (99%)
    pallas_call x1, Pallas kernels, run_chain(): pl.pallas_call(chain_kernel, out_shape=[jax.ShapeDtypeStruct(exchange, BF...  133 us
    pallas_call x1, Pallas kernels, place(): pl.pallas_call(place_kernel, in_specs=[pl.BlockSpec(memory_space=pltpu.HB...  4.6 us

profile of v5, /device:TPU:1, one launch (start us, length us, event | category | flops | bytes accessed | tf_op | source)
XLA Modules:
  0.0 138.0 jit_solution(15830582783649706861)
XLA Ops:
  0.6 132.7 %chain.1 = (bf16[2,32,96,128]{3,2,1,0:T(8,128)(2,1)}, f32[64,128]{1,0:T(8,128)}) custom-call(bf16[256,5120]{1,0:T(8,128)(2,1)} %bitcast.19, bf16[256,5120]{1,0:T(8,128)(2,1)} %bitcast.20, f32[1,5120]{1,0:T(1,128)} %gains.1, bf16[5120,512]{1,0:T(8,128)(2,1)} %bitcast.17, bf16[512,5120]{1,0:T(8,128)(2,1)} %bitcast.18, bf16[160,64,128]{2,1,0:T(8,128)(2,1)} %bitcast.21, ...), custom_call_target="tpu_custom_call" | custom-call | tf_op jit(solution)/shard_map/chain/pallas_call | solution.py:485
  133.4 4.6 %place.1 = (f32[160,64,128]{2,1,0:T(8,128)}, f32[16,64,128]{2,1,0:T(8,128)}) custom-call(f32[64,128]{1,0:T(8,128)} %get-tuple-element.6.picks, bf16[64,96,128]{2,1,0:T(8,128)(2,1)} %bitcast.22), custom_call_target="tpu_custom_call" | custom-call | tf_op jit(solution)/shard_map/place/pallas_call | solution.py:593

commit v6 on v5

--- a/solution.py
+++ b/solution.py
@@ -10,6 +10,7 @@
 TILE = 512
 GROUP = 16
 PIECES = 2
+SENDS = 1
 LANES = 128
 BF16 = jnp.bfloat16
 F32 = jnp.float32
@@ -43,14 +44,18 @@
 def chain_kernel(
     tokens,
     cotangent,
-    gains,
+    gains_whole,
     w_value,
     w_out,
     down,
     up,
+    criterion_whole,
+    slot_of_whole,
+    grad_recv,
+    picks_out,
+    gains,
     criterion,
     slot_of,
-    grad_recv,
     picks,
     value_ref,
     out_ref,
@@ -76,6 +81,7 @@
     product_up,
     grad_send,
     load_sem,
+    down_sem,
     h_send_sem,
     h_recv_sem,
     g_send_sem,
@@ -102,18 +108,43 @@
     packed = panel_send.shape[2]
     value_width = value_grad.shape[1]
     piece_width = width // PIECES
-    pieces = [slice(start, start + piece_width) for start in range(0, width, piece_width)]
+    send_width = width // SENDS
+    sends = [slice(start, start + send_width) for start in range(0, width, send_width)]
     first = section == 0
     last = section == sections - 1
 
     loads = [
         pltpu.make_async_copy(source, target, load_sem.at[place])
         for place, (source, target) in enumerate(
-            [(down, down_ref), (up, up_ref), (w_value, value_ref), (w_out, out_ref)]
+            [
+                (criterion_whole, criterion),
+                (slot_of_whole, slot_of),
+                (up, up_ref),
+                (gains_whole, gains),
+                (w_value, value_ref),
+                (w_out, out_ref),
+                (picks, picks_out),
+            ]
         )
+    ]
+    halves = [
+        [
+            pltpu.make_async_copy(
+                down.at[pl.ds(side * down_half + start, GROUP)],
+                down_ref.at[pl.ds(side * down_half + start, GROUP)],
+                down_sem.at[side, start // GROUP],
+            )
+            for side in range(2)
+        ]
+        for start in range(0, down_half, GROUP)
     ]
     loads[0].start()
     loads[1].start()
+    for both in halves:
+        for load in both:
+            load.start()
+    loads[2].start()
+    loads[3].start()
 
     def tiles_of(piece):
         base = piece * piece_width
@@ -142,36 +173,17 @@
             device_id_type=pl.DeviceIdType.MESH,
         )
 
-    fill_picks(picks, criterion, slot_of)
-    chosen = picks[...].astype(BF16)
     loads[0].wait()
     loads[1].wait()
-    loads[2].start()
-
-    @pl.when(first)
-    def _():
-        for c in range(chunks):
-            part = pl.ds(c * CHUNK, CHUNK)
-            for piece in range(PIECES):
-                pltpu.make_async_copy(
-                    tokens.at[part, pieces[piece]],
-                    h_in.at[part, pieces[piece]],
-                    h_recv_sem.at[c, piece],
-                ).start()
-
-    @pl.when(last)
-    def _():
-        for c in range(chunks):
-            part = pl.ds(c * CHUNK, CHUNK)
-            for piece in range(PIECES):
-                pltpu.make_async_copy(
-                    cotangent.at[part, pieces[piece]],
-                    g_in.at[part, pieces[piece]],
-                    g_recv_sem.at[c, piece],
-                ).start()
-
-    loads[3].start()
+    fill_picks(picks, criterion, slot_of)
+    loads[6].start()
+    chosen = picks[...].astype(BF16)
+    loads[4].start()
+
+    loads[5].start()
     for start in range(0, down_half, GROUP):
+        for load in halves[start // GROUP]:
+            load.wait()
         pair = jnp.concatenate(
             [down_ref[start : start + GROUP], down_ref[down_half + start : down_half + start + GROUP]],
             axis=1,
@@ -179,6 +191,7 @@
         found = dot_nt(chosen, pair.reshape(GROUP * LANES, slots))
         found = found.reshape(micro, peers, GROUP, LANES).astype(BF16)
         panel_send[:, :, start : start + GROUP, :] = found
+    loads[2].wait()
     pair = jnp.concatenate([up_ref[0:up_half], up_ref[up_half:value_rows]], axis=1)
     found = dot_nt(chosen, pair.reshape(up_half * LANES, slots)).reshape(
         micro, peers, up_half, LANES
@@ -219,7 +232,30 @@
 
     spread_panels(0)
 
-    loads[2].wait()
+    @pl.when(first)
+    def _():
+        for c in range(chunks):
+            part = pl.ds(c * CHUNK, CHUNK)
+            for piece in range(SENDS):
+                pltpu.make_async_copy(
+                    tokens.at[part, sends[piece]],
+                    h_in.at[part, sends[piece]],
+                    h_recv_sem.at[c, piece],
+                ).start()
+
+    @pl.when(last)
+    def _():
+        for c in range(chunks):
+            part = pl.ds(c * CHUNK, CHUNK)
+            for piece in range(SENDS):
+                pltpu.make_async_copy(
+                    cotangent.at[part, sends[piece]],
+                    g_in.at[part, sends[piece]],
+                    g_recv_sem.at[c, piece],
+                ).start()
+
+    loads[3].wait()
+    loads[4].wait()
 
     near = lax.broadcasted_iota(jnp.int32, (down_half, LANES), 1) < LANES // 2
     near_up = near[0:up_half]
@@ -245,13 +281,17 @@
 
         lax.fori_loop(0, peers // 2, one, 0)
 
-        @pl.when(m < micro - 1)
+        @pl.when((section > 0) & (m < micro - 1))
         def _():
             spread_panels(m + 1)
+
+    def wait_piece(ref, sem, c, piece):
+        for index in range(SENDS) if piece == 0 else []:
+            wait_for(ref.at[chunk_rows(c), sends[index]], sem.at[c, index])
 
     def send_piece(source, target, c, piece, send_sem, recv_sem, to):
         here = chunk_rows(c)
-        columns = pieces[piece]
+        columns = sends[piece]
         pltpu.make_async_remote_copy(
             src_ref=source.at[here, columns],
             dst_ref=target.at[here, columns],
@@ -273,7 +313,7 @@
         mixed = jnp.zeros((CHUNK, value_width), F32)
         narrow = jnp.zeros((2 * CHUNK, LANES), F32)
         for piece in range(PIECES):
-            wait_for(h_in.at[here, pieces[piece]], h_recv_sem.at[c, piece])
+            wait_piece(h_in, h_recv_sem, c, piece)
             for tile in tiles_of(piece):
                 hidden = h_in[here, tile].astype(F32)
                 square = hidden * hidden
@@ -302,13 +342,15 @@
                 for tile in tiles_of(piece):
                     added = dot(values, out_ref[:, tile])
                     h_out[here, tile] = (h_in[here, tile].astype(F32) + added).astype(BF16)
-                send_piece(h_out, h_in, c, piece, h_send_sem, h_recv_sem, section + 1)
+                    if tile.stop % send_width == 0:
+                        done = tile.stop // send_width - 1
+                        send_piece(h_out, h_in, c, done, h_send_sem, h_recv_sem, section + 1)
 
     def pull(c, carry):
         here = chunk_rows(c)
         pulled = jnp.zeros((CHUNK, value_width), F32)
         for piece in range(PIECES):
-            wait_for(g_in.at[here, pieces[piece]], g_recv_sem.at[c, piece])
+            wait_piece(g_in, g_recv_sem, c, piece)
             for tile in tiles_of(piece):
                 pulled += dot(g_in[here, tile], out_turned[tile, :])
         value_grad[here, :] = pulled.astype(BF16)
@@ -355,7 +397,9 @@
                         - h_in[here, tile].astype(F32) * bend
                     )
                     g_out[here, tile] = result.astype(BF16)
-                send_piece(g_out, g_in, c, piece, g_send_sem, g_recv_sem, section - 1)
+                    if tile.stop % send_width == 0:
+                        done = tile.stop // send_width - 1
+                        send_piece(g_out, g_in, c, done, g_send_sem, g_recv_sem, section - 1)
 
     def products(m):
         here = pl.ds(pl.multiple_of(m * block, block), block)
@@ -405,7 +449,7 @@
     lag = jnp.where(first, chunks, jnp.where(last, 0, (sections - 1 - section) * 3 + (2 - section)))
     lag = jnp.minimum(lag, chunks)
 
-    loads[3].wait()
+    loads[5].wait()
     turn_at = jnp.where(first, chunks, 0)
 
     drawn = jnp.minimum(jnp.maximum(lag + per_block, chunks + 1), chunks + lag) - 1
@@ -419,6 +463,10 @@
         @pl.when((section > 0) & ((t == 0) | (t == per_block // 2)))
         def _():
             unpack(jnp.where(t == 0, 0, 1))
+
+        @pl.when(first & (t == per_block // 2 - 1))
+        def _():
+            spread_panels(1)
 
         @pl.when(t < chunks)
         def _():
@@ -445,6 +493,8 @@
         return carry
 
     lax.fori_loop(0, chunks + lag, step, 0)
+
+    loads[6].wait()
 
     for m in range(micro):
         wait_for(grad_recv.at[m], grad_recv_sem.at[m])
@@ -454,15 +504,15 @@
     @pl.when(section < sections - 1)
     def _():
         for c in range(chunks):
-            for piece in range(PIECES):
-                part = h_out.at[pl.ds(c * CHUNK, CHUNK), pieces[piece]]
+            for piece in range(SENDS):
+                part = h_out.at[pl.ds(c * CHUNK, CHUNK), sends[piece]]
                 wait_for(part, h_send_sem.at[c, piece])
 
     @pl.when(section > 0)
     def _():
         for c in range(chunks):
-            for piece in range(PIECES):
-                part = g_out.at[pl.ds(c * CHUNK, CHUNK), pieces[piece]]
+            for piece in range(SENDS):
+                part = g_out.at[pl.ds(c * CHUNK, CHUNK), sends[piece]]
                 wait_for(part, g_send_sem.at[c, piece])
 
 
@@ -476,10 +526,7 @@
     useful = (down.shape[0] + up.shape[0]) // 2
     packed = (useful + 15) // 16 * 16
     block = rows // micro
-    spaces = [pl.BlockSpec(memory_space=pl.ANY)] * 2
-    spaces += [pl.BlockSpec(memory_space=pltpu.VMEM)]
-    spaces += [pl.BlockSpec(memory_space=pl.ANY)] * 4
-    spaces += [pl.BlockSpec(memory_space=pltpu.SMEM)] * 2
+    spaces = [pl.BlockSpec(memory_space=pl.ANY)] * 9
     row_buffer = pltpu.VMEM((rows, width), BF16)
     exchange = (micro, peers, packed, LANES)
     return pl.pallas_call(
@@ -489,11 +536,12 @@
             jax.ShapeDtypeStruct((micro * criterion.shape[1], slots), F32),
         ],
         in_specs=spaces,
-        out_specs=[
-            pl.BlockSpec(memory_space=pl.ANY),
-            pl.BlockSpec(memory_space=pltpu.VMEM),
-        ],
+        out_specs=[pl.BlockSpec(memory_space=pl.ANY)] * 2,
         scratch_shapes=[
+            pltpu.VMEM(gains.shape, F32),
+            pltpu.SMEM(criterion.shape, jnp.int32),
+            pltpu.SMEM(slot_of.shape, jnp.int32),
+            pltpu.VMEM((micro * criterion.shape[1], slots), F32),
             pltpu.VMEM(w_value.shape, BF16),
             pltpu.VMEM(w_out.shape, BF16),
             pltpu.VMEM(w_out.shape, BF16),
@@ -517,11 +565,12 @@
             pltpu.VMEM((micro, value_width, LANES), BF16),
             pltpu.VMEM((value_width, LANES), F32),
             pltpu.VMEM(exchange, BF16),
-            pltpu.SemaphoreType.DMA((4,)),
-            pltpu.SemaphoreType.DMA((chunks, PIECES)),
-            pltpu.SemaphoreType.DMA((chunks, PIECES)),
-            pltpu.SemaphoreType.DMA((chunks, PIECES)),
-            pltpu.SemaphoreType.DMA((chunks, PIECES)),
+            pltpu.SemaphoreType.DMA((7,)),
+            pltpu.SemaphoreType.DMA((2, down.shape[0] // 2 // GROUP)),
+            pltpu.SemaphoreType.DMA((chunks, SENDS)),
+            pltpu.SemaphoreType.DMA((chunks, SENDS)),
+            pltpu.SemaphoreType.DMA((chunks, SENDS)),
+            pltpu.SemaphoreType.DMA((chunks, SENDS)),
             pltpu.SemaphoreType.DMA((micro,)),
             pltpu.SemaphoreType.DMA((micro, peers)),
             pltpu.SemaphoreType.DMA((micro,)),

time: 138 us -> 136 us (0.986)
  Pallas kernels: 137 us -> 135 us
    pallas_call x1, Pallas kernels: 133 us -> 131 us  [run_chain(): pl.pallas_call(chain_kernel, out_shape=[jax.ShapeDtypeStruct(exchange, BF...]
where the time goes in v6:
time: 136 us
  Pallas kernels  135 us (99%)
    pallas_call x1, Pallas kernels, run_chain(): pl.pallas_call(chain_kernel, out_shape=[jax.ShapeDtypeStruct(exchange, BF...  131 us
    pallas_call x1, Pallas kernels, place(): pl.pallas_call(place_kernel, in_specs=[pl.BlockSpec(memory_space=pltpu.HB...  4.6 us

profile of v6, /device:TPU:1, one launch (start us, length us, event | category | flops | bytes accessed | tf_op | source)
XLA Modules:
  0.0 135.9 jit_solution(12551106816366867729)
XLA Ops:
  0.6 130.7 %chain.1 = (bf16[2,32,96,128]{3,2,1,0:T(8,128)(2,1)}, f32[64,128]{1,0:T(8,128)}) custom-call(bf16[256,5120]{1,0:T(8,128)(2,1)} %bitcast.19, bf16[256,5120]{1,0:T(8,128)(2,1)} %bitcast.20, f32[1,5120]{1,0:T(1,128)} %gains_whole.1, bf16[5120,512]{1,0:T(8,128)(2,1)} %bitcast.17, bf16[512,5120]{1,0:T(8,128)(2,1)} %bitcast.18, bf16[160,64,128]{2,1,0:T(8,128)(2,1)} %bitcast.21, ...), custom_call_target="tpu_custom_call" | custom-call | tf_op jit(solution)/shard_map/chain/pallas_call | solution.py:532
  131.3 4.6 %place.1 = (f32[160,64,128]{2,1,0:T(8,128)}, f32[16,64,128]{2,1,0:T(8,128)}) custom-call(f32[64,128]{1,0:T(8,128)} %get-tuple-element.6.picks, bf16[64,96,128]{2,1,0:T(8,128)(2,1)} %bitcast.22), custom_call_target="tpu_custom_call" | custom-call | tf_op jit(solution)/shard_map/place/pallas_call | solution.py:642

commit v7 on v6

--- a/solution.py
+++ b/solution.py
@@ -301,7 +301,7 @@
             device_id_type=pl.DeviceIdType.MESH,
         ).start()
 
-    def forward(c):
+    def forward(c, onward):
         m = c // per_block
         here = chunk_rows(c)
 
@@ -336,8 +336,7 @@
         low[here, :] = narrow
         values = (mixed * factor + dot_nt(narrow, panel_up[m])).astype(BF16)
 
-        @pl.when(section < sections - 1)
-        def _():
+        if onward:
             for piece in range(PIECES):
                 for tile in tiles_of(piece):
                     added = dot(values, out_ref[:, tile])
@@ -364,42 +363,40 @@
         low_grad[here, :] = (narrow * factor).astype(BF16)
         return narrow.astype(BF16), factor
 
-    def backward(c):
+    def backward(c, drawn_before, onward):
+        here = chunk_rows(c)
+        if not drawn_before:
+            pull(c, 0)
+        pulled = value_grad[here, :]
+        if not onward:
+            lower(c, pulled)
+            return
         m = c // per_block
-        here = chunk_rows(c)
-
-        @pl.when(first)
-        def _():
-            lower(c, value_grad[here, :])
-
-        @pl.when(section > 0)
-        def _():
-            pulled = value_grad[here, :]
-            held, factor = lower(c, pulled)
-            parts = [dot(pulled, value_turned[:, tile]) for tile in tiles_of(0)]
-            along = pulled.astype(F32) * mixed_ref[here, :]
-            moment = jnp.sum(along, axis=1, keepdims=True)
-            along = held.astype(F32) * narrow_ref[here, :]
-            moment += jnp.sum(along, axis=1, keepdims=True)
-            bend = factor * factor * factor * (moment / width)
-            none = jnp.zeros_like(held)
-            both = [jnp.where(near_row, held, none), jnp.where(near_row, none, held)]
-            both = jnp.concatenate(both, axis=0)
-            lifts = [dot_nt(both, panel_down[m, tile, :]) for tile in tiles_of(0)]
-            for piece in range(PIECES):
-                if piece > 0:
-                    parts = [dot(pulled, value_turned[:, tile]) for tile in tiles_of(piece)]
-                for part, lift, tile in zip(parts, lifts, tiles_of(piece)):
-                    part += lift[piece * CHUNK : (piece + 1) * CHUNK]
-                    result = (
-                        g_in[here, tile].astype(F32)
-                        + factor * (part * gains[:, tile])
-                        - h_in[here, tile].astype(F32) * bend
-                    )
-                    g_out[here, tile] = result.astype(BF16)
-                    if tile.stop % send_width == 0:
-                        done = tile.stop // send_width - 1
-                        send_piece(g_out, g_in, c, done, g_send_sem, g_recv_sem, section - 1)
+        held, factor = lower(c, pulled)
+        parts = [dot(pulled, value_turned[:, tile]) for tile in tiles_of(0)]
+        along = pulled.astype(F32) * mixed_ref[here, :]
+        moment = jnp.sum(along, axis=1, keepdims=True)
+        along = held.astype(F32) * narrow_ref[here, :]
+        moment += jnp.sum(along, axis=1, keepdims=True)
+        bend = factor * factor * factor * (moment / width)
+        none = jnp.zeros_like(held)
+        both = [jnp.where(near_row, held, none), jnp.where(near_row, none, held)]
+        both = jnp.concatenate(both, axis=0)
+        lifts = [dot_nt(both, panel_down[m, tile, :]) for tile in tiles_of(0)]
+        for piece in range(PIECES):
+            if piece > 0:
+                parts = [dot(pulled, value_turned[:, tile]) for tile in tiles_of(piece)]
+            for part, lift, tile in zip(parts, lifts, tiles_of(piece)):
+                part += lift[piece * CHUNK : (piece + 1) * CHUNK]
+                result = (
+                    g_in[here, tile].astype(F32)
+                    + factor * (part * gains[:, tile])
+                    - h_in[here, tile].astype(F32) * bend
+                )
+                g_out[here, tile] = result.astype(BF16)
+                if tile.stop % send_width == 0:
+                    done = tile.stop // send_width - 1
+                    send_piece(g_out, g_in, c, done, g_send_sem, g_recv_sem, section - 1)
 
     def products(m):
         here = pl.ds(pl.multiple_of(m * block, block), block)
@@ -468,19 +465,29 @@
         def _():
             spread_panels(1)
 
-        @pl.when(t < chunks)
-        def _():
-            forward(t)
+        @pl.when((t < chunks) & (section < sections - 1))
+        def _():
+            forward(t, True)
+
+        @pl.when((t < chunks) & last)
+        def _():
+            forward(t, False)
 
         c = t - lag
 
-        @pl.when((c >= 0) & (c < chunks))
-        def _():
-            @pl.when(section < sections - 1)
-            def _():
-                pull(c, 0)
-
-            backward(c)
+        live = (c >= 0) & (c < chunks)
+
+        @pl.when(live & first)
+        def _():
+            backward(c, False, False)
+
+        @pl.when(live & (section > 0) & (section < sections - 1))
+        def _():
+            backward(c, False, True)
+
+        @pl.when(live & last)
+        def _():
+            backward(c, True, True)
 
         @pl.when(t == drawn)
         def _():

time: 136 us -> 136 us (level)
  no operation moved by 1% of the time
where the time goes in v7:
time: 136 us
  Pallas kernels  135 us (99%)
    pallas_call x1, Pallas kernels, run_chain(): pl.pallas_call(chain_kernel, out_shape=[jax.ShapeDtypeStruct(exchange, BF...  130 us
    pallas_call x1, Pallas kernels, place(): pl.pallas_call(place_kernel, in_specs=[pl.BlockSpec(memory_space=pltpu.HB...  4.6 us

profile of v7, /device:TPU:1, one launch (start us, length us, event | category | flops | bytes accessed | tf_op | source)
XLA Modules:
  0.0 135.6 jit_solution(6765676257109329923)
XLA Ops:
  0.6 130.3 %chain.1 = (bf16[2,32,96,128]{3,2,1,0:T(8,128)(2,1)}, f32[64,128]{1,0:T(8,128)}) custom-call(bf16[256,5120]{1,0:T(8,128)(2,1)} %bitcast.19, bf16[256,5120]{1,0:T(8,128)(2,1)} %bitcast.20, f32[1,5120]{1,0:T(1,128)} %gains_whole.1, bf16[5120,512]{1,0:T(8,128)(2,1)} %bitcast.17, bf16[512,5120]{1,0:T(8,128)(2,1)} %bitcast.18, bf16[160,64,128]{2,1,0:T(8,128)(2,1)} %bitcast.21, ...), custom_call_target="tpu_custom_call" | custom-call | tf_op jit(solution)/shard_map/chain/pallas_call | solution.py:539
  131.0 4.6 %place.1 = (f32[160,64,128]{2,1,0:T(8,128)}, f32[16,64,128]{2,1,0:T(8,128)}) custom-call(f32[64,128]{1,0:T(8,128)} %get-tuple-element.6.picks, bf16[64,96,128]{2,1,0:T(8,128)(2,1)} %bitcast.22), custom_call_target="tpu_custom_call" | custom-call | tf_op jit(solution)/shard_map/place/pallas_call | solution.py:649
